TPU v7x, 32 devices: a whole 2x2x4 slice. The times are simulated.
32 devices in a mesh: view: 2 (over x), seq: 4 (over y, core), event: 4 (over z).
Axes of the slice: x: 2, y: 2, z: 4, core: 2. Of those that a mesh axis runs over, the one named last changes fastest.
Arguments:
- query: bfloat16 [4, 2, 1536, 512], P('event', 'view', 'seq'), may hold values from -7 to 7
- key: bfloat16 [4, 2, 1536, 512], P('event', 'view', 'seq'), may hold values from -7 to 7
- value: bfloat16 [4, 2, 1536, 512], P('event', 'view', 'seq'), may hold values from -6 to 6
- pattern: int32 [4, 2, 12, 12], P('event', 'view', 'seq'), may hold values from 0 to 1, as said below
- out_weight: bfloat16 [512, 512], replicated, may hold values from -0.25 to 0.25
- served: int32 [4, 2, 32, 128], P('event', 'view', 'seq'), may hold values from 0 to 383
- anchor_rows: int32 [4, 2, 1024], P('event', 'view', 'seq'), may hold values from 0 to 383
- positive_slot: int32 [4, 2, 1024], P('event', 'view', 'seq'), may hold values from 0 to 1023, as said below
- anchor_live: int32 [4, 2, 1024], P('event', 'view', 'seq'), may hold values from 0 to 1, as said below
Outputs:
- mixed: bfloat16 [4, 2, 1536, 512], P('event', 'view', 'seq')
- grad_wo: float32 [512, 512], replicated
- loss: float32 [], replicated
Inputs may be any that keep to these rules, and one draw needn't show every extreme that they name: pattern[e, v, b, b] is 1 for every block b. `positive_slot`: for an anchor of view v the slot lies in [(1 - v) * 512, (2 - v) * 512), a point of the other view. `anchor_live`: every device's block of 256 anchors holds at least one live anchor.
All inputs are finite; a program needn't handle non-finite values.
Results may differ from a plain program's by a relative error of at most 0.015.
Values may be sent and summed in bfloat16 or wider, within the bound.
A program may use at most 64 MiB of HBM per device.

v0:
```python
import jax
import jax.numpy as jnp
from jax import lax
from jax.sharding import PartitionSpec as P

HEADS = 16
BLOCK = 128


NEGATIVE = -1e30
SHARPNESS_SCALE = 0.07


def from_behind(array, axis, by):
    peers = lax.axis_size(axis)
    return lax.ppermute(array, axis, [(i, (i + by) % peers) for i in range(peers)])


def per_device(
    query, key, value, pattern, out_weight, served, anchor_rows, positive_slot, anchor_live
):
    queries = query[0, 0]
    keys = key[0, 0]
    values = value[0, 0]
    points, width = queries.shape
    head_dim = width // HEADS
    scale = head_dim ** (-0.5)
    loop_size = lax.axis_size("seq")
    myself = lax.axis_index("seq")
    local_pattern = pattern[0, 0].astype(jnp.float32)
    blocks_dev, blocks_all = local_pattern.shape
    query_block = jnp.arange(points) // BLOCK
    pick_rows = (query_block[:, None] == jnp.arange(blocks_dev)[None, :]).astype(jnp.float32)
    row_pattern = jnp.dot(pick_rows, local_pattern, preferred_element_type=jnp.float32)
    head_queries = queries.reshape(points, HEADS, head_dim)

    def attend(state, key_piece, value_piece, start):
        length = key_piece.shape[0]
        count = length // BLOCK
        size = BLOCK
        key_groups = key_piece.reshape(count, size, width)
        value_groups = value_piece.reshape(count, size, width)
        offsets = start + jnp.arange(count, dtype=jnp.int32) * size

        def one_group(carry, inputs):
            key_group, value_group, offset = inputs
            key_block = (offset + jnp.arange(size)) // BLOCK
            pick_keys = (jnp.arange(blocks_all)[:, None] == key_block[None, :]).astype(jnp.float32)
            allowed = jnp.dot(row_pattern, pick_keys, preferred_element_type=jnp.float32) > 0.5
            best, total, accum = carry
            head_keys = key_group.reshape(size, HEADS, head_dim)
            head_values = value_group.reshape(size, HEADS, head_dim)
            scores = (
                jnp.einsum(
                    "qhd,khd->hqk", head_queries, head_keys, preferred_element_type=jnp.float32
                )
                * scale
            )
            scores = jnp.where(allowed[None], scores, NEGATIVE)
            new_best = jnp.maximum(best, jnp.max(scores, axis=-1))
            weights = jnp.where(allowed[None], jnp.exp(scores - new_best[..., None]), 0.0)
            factor = jnp.exp(best - new_best)
            total = total * factor + jnp.sum(weights, axis=-1)
            added = jnp.einsum(
                "hqk,khd->hqd",
                weights.astype(jnp.bfloat16),
                head_values,
                preferred_element_type=jnp.float32,
            )
            result = (new_best, total, accum * factor[..., None] + added)
            return (result, None)

        final_state, unused = lax.scan(one_group, state, (key_groups, value_groups, offsets))
        return final_state

    initial = (
        jnp.full((HEADS, points), NEGATIVE, jnp.float32),
        jnp.zeros((HEADS, points), jnp.float32),
        jnp.zeros((HEADS, points, head_dim), jnp.float32),
    )
    state = attend(initial, keys, values, myself * points)
    moving = (keys, values)
    for step in range(1, loop_size):
        moving = from_behind((moving[0], moving[1]), "seq", 1)
        root = (myself - step) % loop_size
        state = attend(state, moving[0], moving[1], root * points)
    best, total, accum = state
    mixed = (
        (accum / total[..., None]).transpose(1, 0, 2).reshape(points, width).astype(jnp.bfloat16)
    )
    embedding_rows = jnp.dot(mixed, out_weight, preferred_element_type=jnp.float32)
    inverse = lax.rsqrt(jnp.sum(embedding_rows * embedding_rows, axis=-1) + 1e-06)
    unit = (embedding_rows * inverse[:, None]).astype(jnp.bfloat16)
    served_rows = served[0, 0]
    senders, capacity = served_rows.shape
    flat_served = served_rows.reshape(-1)
    outgoing = jnp.take(unit, flat_served, axis=0).reshape(senders, capacity, width)
    incoming = lax.all_to_all(outgoing, ("view", "seq"), split_axis=0, concat_axis=0, tiled=True)
    contender_vectors = incoming.reshape(senders * capacity, width)
    own_rows = anchor_rows[0, 0]
    query_vectors = jnp.take(unit, own_rows, axis=0)
    pairwise_scores = (
        lax.dot_general(
            query_vectors,
            contender_vectors,
            (((1,), (1,)), ((), ())),
            preferred_element_type=jnp.float32,
        )
        / SHARPNESS_SCALE
    )
    exponentiated_scores = jnp.exp(pairwise_scores)
    partition_totals = jnp.sum(exponentiated_scores, axis=-1)
    log_total = jnp.log(partition_totals)
    correct_column = (
        jnp.arange(senders * capacity)[None, :] == positive_slot[0, 0][:, None]
    ).astype(jnp.float32)
    active_queries = anchor_live[0, 0].astype(jnp.float32)
    loss_part = jnp.sum(
        active_queries * (log_total - jnp.sum(pairwise_scores * correct_column, axis=-1))
    )
    live_part = jnp.sum(active_queries)
    score_derivatives = (
        active_queries[:, None]
        * (exponentiated_scores / partition_totals[:, None] - correct_column)
        / SHARPNESS_SCALE
    )
    anchor_grads = jnp.dot(
        score_derivatives, contender_vectors.astype(jnp.float32), precision=lax.Precision.HIGHEST
    )
    candidate_grads = lax.dot_general(
        score_derivatives,
        query_vectors.astype(jnp.float32),
        (((0,), (0,)), ((), ())),
        precision=lax.Precision.HIGHEST,
    )
    returned = lax.all_to_all(
        candidate_grads.reshape(senders, capacity, width).astype(jnp.bfloat16),
        ("view", "seq"),
        split_axis=0,
        concat_axis=0,
        tiled=True,
    ).astype(jnp.float32)
    unit_grads = (
        jnp.zeros((points, width), jnp.float32).at[flat_served].add(returned.reshape(-1, width))
    )
    unit_grads = unit_grads.at[own_rows].add(anchor_grads)
    inner = jnp.sum(embedding_rows * unit_grads, axis=-1)
    embedding_gradients = (
        inverse[:, None] * (unit_grads - embedding_rows * (inverse * inverse * inner)[:, None])
    ).astype(jnp.bfloat16)
    loss_term = lax.dot_general(
        mixed, embedding_gradients, (((0,), (0,)), ((), ())), preferred_element_type=jnp.float32
    )
    grad_total, loss_total, live_total = lax.psum(
        (loss_term, loss_part, live_part), ("view", "seq", "event")
    )
    return (mixed[None, None], grad_total, loss_total / live_total)


def solution(mesh):
    placed = (
        P("event", "view", "seq", None),
        P("event", "view", "seq", None),
        P("event", "view", "seq", None),
        P("event", "view", "seq", None),
        P(),
        P("event", "view", "seq", None),
        P("event", "view", "seq"),
        P("event", "view", "seq"),
        P("event", "view", "seq"),
    )
    return jax.shard_map(
        per_device,
        mesh=mesh,
        in_specs=placed,
        out_specs=(P("event", "view", "seq", None), P(), P()),
        check_vma=False,
    )
```

profile of v0, /device:TPU:0, one launch (start us, length us, event | category | flops | bytes accessed | tf_op | source)
XLA Modules:
  0.0 321.7 jit_solution(7851278971692697415)
XLA Ops:
  7.7 2.6 collective-permute-start.1
  12.5 31.9 %while.68 = (s32[]{:T(128)}, f32[16,384]{1,0:T(8,128)S(1)}, f32[16,384]{1,0:T(8,128)S(1)}, f32[16,384,32]{1,2,0:T(8,128)S(1)}, s32[3]{0:T(128)S(1)}, /*index=5*/...) while((s32[]{:T(128)}, f32[16,384]{1,0:T(8,128)S(1)}, ...), condition=%wide.region_3.4_spmd.clone, body=%wide.region_0.3_spmd.clone.sunk | while | flops 112739840 | bytes 13314189 | solution.py:73
  15.1 2.3 fusion.168
  17.5 2.7 fusion.169
  20.3 2.8 fusion.171
  25.7 2.3 fusion.168
  28.1 2.7 fusion.169
  30.9 2.8 fusion.171
  38.7 2.7 fusion.169
  41.5 2.8 fusion.171
  45.2 26.6 %while.65 = (s32[]{:T(128)}, f32[16,384]{1,0:T(8,128)S(1)}, f32[16,384]{1,0:T(8,128)S(1)}, f32[16,384,32]{1,2,0:T(8,128)S(1)}, s32[3]{0:T(128)S(1)}, /*index=5*/...) while((s32[]{:T(128)}, f32[16,384]{1,0:T(8,128)S(1)}, ...), condition=%wide.region_7.8_spmd, body=%wide.region_4.7_spmd.sunk | while | flops 112524800 | bytes 25897108 | solution.py:73
  51.2 2.8 fusion.143
  60.1 2.8 fusion.143
  69.0 2.8 fusion.143
  73.9 26.6 %while.66 = (s32[]{:T(128)}, f32[16,384]{1,0:T(8,128)S(1)}, f32[16,384]{1,0:T(8,128)S(1)}, f32[16,384,32]{1,2,0:T(8,128)S(1)}, s32[3]{0:T(128)S(1)}, /*index=5*/...) while((s32[]{:T(128)}, f32[16,384]{1,0:T(8,128)S(1)}, ...), condition=%wide.region_11.12_spmd, body=%wide.region_8.11_spmd.sunk | while | flops 112524800 | bytes 25897108 | solution.py:73
  80.0 2.8 fusion.152
  88.8 2.8 fusion.152
  97.7 2.8 fusion.152
  100.5 23.4 %while.67 = (s32[]{:T(128)}, f32[16,384]{1,0:T(8,128)S(1)}, f32[16,384]{1,0:T(8,128)S(1)}, f32[16,384,32]{1,2,0:T(8,128)S(1)}, s32[3]{0:T(128)S(1)}, /*index=5*/...) while((s32[]{:T(128)}, f32[16,384]{1,0:T(8,128)S(1)}, ...), condition=%wide.region_15.16_spmd, body=%wide.region_12.15_spmd.sunk | while | flops 112524800 | bytes 25897108 | solution.py:73
  105.5 2.8 fusion.161
  113.3 2.8 fusion.161
  121.1 2.8 fusion.161
  124.6 4.0 %gather_fusion.1 = bf16[1024,512]{1,0:T(8,128)(2,1)S(1)} fusion(bf16[384,512]{1,0:T(8,128)(2,1)S(1)} %multiply_convert_fusion.1, s32[1024]{0:T(1024)S(1)} %broadcast_clamp_fusion), kind=kCustom, calls=%fused_computation.1 | custom fusion | bytes 2101248 | tf_op jit(solution)/shard_map/jit(_take)/gather | solution.py:97
  129.8 3.6 %all-to-all-start = ((bf16[8,128,512]{2,1,0:T(8,128)(2,1)}), bf16[8,128,512]{2,1,0:T(8,128)(2,1)S(1)}, u32[]{:S(2)}, u32[]{:S(2)}) async-start(bf16[8,128,512]{2,1,0:T(8,128)(2,1)} %broadcast_select_fusion), calls=%async_computation | async-start | bytes 2097152 | tf_op jit(solution)/shard_map/all_to_all | solution.py:98
  134.6 13.1 %all-to-all-done = bf16[8,128,512]{2,1,0:T(8,128)(2,1)S(1)} async-done(((bf16[8,128,512]{2,1,0:T(8,128)(2,1)}), bf16[8,128,512]{2,1,0:T(8,128)(2,1)S(1)}, u32[]{:S(2)}, u32[]{:S(2)}) %all-to-all-start) | async-done | bytes 1048608 | tf_op jit(solution)/shard_map/all_to_all | solution.py:98
  151.3 3.6 %all-to-all-start.1 = ((bf16[8,128,512]{2,1,0:T(8,128)(2,1)}), bf16[8,128,512]{2,1,0:T(8,128)(2,1)S(1)}, u32[]{:S(2)}, u32[]{:S(2)}) async-start(bf16[8,128,512]{2,1,0:T(8,128)(2,1)} %bitcast.239), calls=%async_computation.1 | async-start | bytes 2097152 | tf_op jit(solution)/shard_map/all_to_all | solution.py:136
  155.2 3.6 %fusion.76 = f32[256,512]{1,0:T(8,128)} fusion(bf16[1024,512]{1,0:T(8,128)(2,1)} %bitcast.238, f32[256,1024]{1,0:T(8,128)} %copy-done.16, s32[256]{0:T(256)S(1)} %bitcast.251, f32[256]{0:T(256)S(1)} %get-tuple-element.547, f32[256]{0:T(256)S(1)} %bitcast.246), kind=kOutput, calls=%fused_computation.149 | convolution fusion | flops 1612185600 | bytes 2624512 | tf_op jit(solution)/shard_map/dot_general | solution.py:127
  158.7 10.5 %all-to-all-done.1 = bf16[8,128,512]{2,1,0:T(8,128)(2,1)S(1)} async-done(((bf16[8,128,512]{2,1,0:T(8,128)(2,1)}), bf16[8,128,512]{2,1,0:T(8,128)(2,1)S(1)}, u32[]{:S(2)}, u32[]{:S(2)}) %all-to-all-start.1) | async-done | bytes 1048608 | tf_op jit(solution)/shard_map/all_to_all | solution.py:136
  169.3 6.9 %scatter_custom_fusion = f32[384,512]{1,0:T(8,128)S(1)} fusion(s32[1024]{0:T(1024)S(1)} %bitcast.242, bf16[1024,512]{1,0:T(8,128)(2,1)S(1)} %bitcast.226, f32[]{:T(128)} %constant.342.clone.1), kind=kCustom, calls=%fused_computation.99 | custom fusion | flops 1048576 | bytes 1835012 | tf_op jit(solution)/shard_map/scatter-add | solution.py:144
  176.2 2.9 scatter_fusion
  183.1 40.1 %all-reduce = (f32[]{:T(128)}, f32[]{:T(128)}) all-reduce(f32[]{:T(128)} %multiply_reduce_fusion.2, f32[]{:T(128)} %convert_reduce_fusion), channel_id=1, replica_groups=mesh['view'=2,'seq'=4,'event'=4] {'view','seq','event'}, use_global_device_ids=true, to_apply=%region_24.25 | all-reduce | flops 2 | bytes 16 | tf_op jit(solution)/shard_map/psum | solution.py:154
  224.6 86.9 %all-reduce.3.cloned.1.call-done = f32[512,512]{1,0:T(8,128)} async-done(((f32[512,512]{1,0:T(8,128)}), f32[512,512]{1,0:T(8,128)}) %all-reduce.3.cloned.1.call-update) | async-done | bytes 1048592 | tf_op jit(solution)/shard_map/psum | solution.py:154
  (219 shorter events, 79.7 us)
Async XLA Ops:
  7.2 116.8 %copy-start = (bf16[512,512]{1,0:T(8,128)(2,1)S(1)}, bf16[512,512]{1,0:T(8,128)(2,1)}, u32[]{:S(2)}) copy-start(bf16[512,512]{1,0:T(8,128)(2,1)} %param.21) | copy-start | bytes 1572868
  7.2 37.8 %collective-permute-start = (bf16[384,512]{1,0:T(8,128)(2,1)}, bf16[384,512]{1,0:T(8,128)(2,1)}, u32[]{:S(2)}, u32[]{:S(2)}) collective-permute-start(bf16[384,512]{1,0:T(8,128)(2,1)} %bitcast.231), channel_id=1, source_target_pairs={{0,4},{4,8},{8,12},{12,0},{1,5},{5,9},{9,13},{13,1},{2,6},{6,10},{... | collective-permute-start | bytes 1179656 | tf_op jit(solution)/shard_map/ppermute | solution.py:16
  7.7 37.4 %collective-permute-start.1 = (bf16[384,512]{1,0:T(8,128)(2,1)}, bf16[384,512]{1,0:T(8,128)(2,1)}, u32[]{:S(2)}, u32[]{:S(2)}) collective-permute-start(bf16[384,512]{1,0:T(8,128)(2,1)} %bitcast.233), channel_id=1, source_target_pairs={{0,4},{4,8},{8,12},{12,0},{1,5},{5,9},{9,13},{13,1},{2,6},{6,10},{... | collective-permute-start | bytes 1179656 | tf_op jit(solution)/shard_map/ppermute | solution.py:16
  12.5 31.9 %copy-start.5 = (s32[1,1,8,128]{3,2,1,0:T(8,128)S(1)}, s32[1,1,8,128]{3,2,1,0:T(8,128)}, u32[]{:S(2)}) copy-start(s32[1,1,8,128]{3,2,1,0:T(8,128)} %param.22) | copy-start | bytes 12292
  45.0 26.8 %collective-permute-start.2 = (bf16[384,512]{1,0:T(8,128)(2,1)}, bf16[384,512]{1,0:T(8,128)(2,1)}, u32[]{:S(2)}, u32[]{:S(2)}) collective-permute-start(bf16[384,512]{1,0:T(8,128)(2,1)} %collective-permute-done), channel_id=1, source_target_pairs={{0,4},{4,8},{8,12},{12,0},{1,5},{5,9},{9,13},{13,1},{2,6},{6,10},{... | collective-permute-start | bytes 1179656 | tf_op jit(solution)/shard_map/ppermute | solution.py:16
  45.1 26.9 %collective-permute-start.3 = (bf16[384,512]{1,0:T(8,128)(2,1)}, bf16[384,512]{1,0:T(8,128)(2,1)}, u32[]{:S(2)}, u32[]{:S(2)}) collective-permute-start(bf16[384,512]{1,0:T(8,128)(2,1)} %collective-permute-done.1), channel_id=1, source_target_pairs={{0,4},{4,8},{8,12},{12,0},{1,5},{5,9},{9,13},{13,1},{2,6},{6,10},{... | collective-permute-start | bytes 1179656 | tf_op jit(solution)/shard_map/ppermute | solution.py:16
  48.6 1.7 copy-start.1
  57.5 1.7 copy-start.1
  66.3 1.7 copy-start.1
  71.8 28.7 %collective-permute-start.4 = (bf16[384,512]{1,0:T(8,128)(2,1)}, bf16[384,512]{1,0:T(8,128)(2,1)S(1)}, u32[]{:S(2)}, u32[]{:S(2)}) collective-permute-start(bf16[384,512]{1,0:T(8,128)(2,1)} %collective-permute-done.2), channel_id=1, source_target_pairs={{0,4},{4,8},{8,12},{12,0},{1,5},{5,9},{9,13},{13,1},{2,6},{6,10},{... | collective-permute-start | bytes 1179656 | tf_op jit(solution)/shard_map/ppermute | solution.py:16
  71.9 28.6 %collective-permute-start.5 = (bf16[384,512]{1,0:T(8,128)(2,1)}, bf16[384,512]{1,0:T(8,128)(2,1)S(1)}, u32[]{:S(2)}, u32[]{:S(2)}) collective-permute-start(bf16[384,512]{1,0:T(8,128)(2,1)} %collective-permute-done.3), channel_id=1, source_target_pairs={{0,4},{4,8},{8,12},{12,0},{1,5},{5,9},{9,13},{13,1},{2,6},{6,10},{... | collective-permute-start | bytes 1179656 | tf_op jit(solution)/shard_map/ppermute | solution.py:16
  77.3 1.7 copy-start.2
  86.2 1.7 copy-start.2
  95.1 1.7 copy-start.2
  102.9 1.7 copy-start.3
  110.7 1.7 copy-start.3
  118.5 1.7 copy-start.3
  124.6 4.0 %copy-start.6 = (pred[8,128]{1,0:T(8,128)(4,1)S(1)}, pred[8,128]{1,0:T(8,128)(4,1)}, u32[]{:S(2)}) copy-start(pred[8,128]{1,0:T(8,128)(4,1)} %compare_and_fusion) | copy-start | bytes 3076
  128.6 4.8 %copy-start.13 = (s32[1,1,256]{2,1,0:T(1,128)S(1)}, s32[1,1,256]{2,1,0:T(1,128)}, u32[]{:S(2)}) copy-start(s32[1,1,256]{2,1,0:T(1,128)} %param.25) | copy-start | bytes 3076
  128.6 4.8 %copy-start.12 = (s32[1,1,256]{2,1,0:T(1,128)S(1)}, s32[1,1,256]{2,1,0:T(1,128)}, u32[]{:S(2)}) copy-start(s32[1,1,256]{2,1,0:T(1,128)} %param.23) | copy-start | bytes 3076
  128.7 19.1 %copy-start.15 = (s32[1,1,256]{2,1,0:T(1,128)S(1)}, s32[1,1,256]{2,1,0:T(1,128)}, u32[]{:S(2)}) copy-start(s32[1,1,256]{2,1,0:T(1,128)} %param.24) | copy-start | bytes 3076
  129.8 17.9 %all-to-all-start = ((bf16[8,128,512]{2,1,0:T(8,128)(2,1)}), bf16[8,128,512]{2,1,0:T(8,128)(2,1)S(1)}, u32[]{:S(2)}, u32[]{:S(2)}) async-start(bf16[8,128,512]{2,1,0:T(8,128)(2,1)} %broadcast_select_fusion), calls=%async_computation | async-start | bytes 2097152 | tf_op jit(solution)/shard_map/all_to_all | solution.py:98
  133.4 21.7 %copy-start.7 = (f32[1,1,256]{2,1,0:T(1,128)}, f32[1,1,256]{2,1,0:T(1,128)S(1)}, u32[]{:S(2)}) copy-start(f32[1,1,256]{2,1,0:T(1,128)S(1)} %convert_element_type.89) | copy-start | bytes 3076
  147.8 3.5 %copy-start.4 = (bf16[8,128,512]{2,1,0:T(8,128)(2,1)}, bf16[8,128,512]{2,1,0:T(8,128)(2,1)S(1)}, u32[]{:S(2)}) copy-start(bf16[8,128,512]{2,1,0:T(8,128)(2,1)S(1)} %all-to-all-done) | copy-start | bytes 3145732
  149.0 2.3 copy-start.16
  149.0 6.1 %copy-start.10 = (f32[256]{0:T(256)}, f32[256]{0:T(256)S(1)}, u32[]{:S(2)}) copy-start(f32[256]{0:T(256)S(1)} %get-tuple-element.547) | copy-start | bytes 3076
  151.3 17.9 %all-to-all-start.1 = ((bf16[8,128,512]{2,1,0:T(8,128)(2,1)}), bf16[8,128,512]{2,1,0:T(8,128)(2,1)S(1)}, u32[]{:S(2)}, u32[]{:S(2)}) async-start(bf16[8,128,512]{2,1,0:T(8,128)(2,1)} %bitcast.239), calls=%async_computation.1 | async-start | bytes 2097152 | tf_op jit(solution)/shard_map/all_to_all | solution.py:136
  154.9 156.6 %all-reduce.3.cloned.1.call-start = ((), (), s32[]{:S(2)}) async-start(), calls=%async_computation.2 | async-start | bytes 2097152 | tf_op jit(solution)/shard_map/psum | solution.py:154
  179.1 1.8 copy-start.14
  179.1 2.4 copy-start.8
  179.1 2.4 copy-start.9
  179.1 2.4 copy-start.11
Sparse Core Ops, SparseCore 0:
  181.0 130.4 all-reduce.2
where the time goes:
time: 323 us; the launch traced here: 322 us
  waiting for transfers between devices  111 us (34%)
  matrix products  59 us (18%)
  local copies, waits for them, and re-layouts  43.9 us (14%)
  blocking collectives  40.1 us (12%)
  other arithmetic  37.4 us (12%)
  between operations  16.9 us (5%)
  starting transfers between devices  12.8 us (4%)
    psum x1, waiting for transfers between devices, per_device(): lax.psum((loss_term, loss_part, live_part), ('view', 'seq', 'event'))  86.9 us
    psum x1, blocking collectives, per_device(): lax.psum((loss_term, loss_part, live_part), ('view', 'seq', 'event'))  40.1 us
    dot_general x12, matrix products, one_group(): jnp.einsum('hqk,khd->hqd', weights.astype(jnp.bfloat16), head_values, pre...  33.7 us
    dynamic_slice x48, local copies, waits for them, and re-layouts, attend(): lax.scan(one_group, state, (key_groups, value_groups, offsets))  19.4 us
    reduce_sum x12, other arithmetic, one_group(): total = total * factor + jnp.sum(weights, axis=-1)  15.1 us
    while x30, local copies, waits for them, and re-layouts  14.8 us
    dot_general x12, matrix products, one_group(): jnp.einsum('qhd,khd->hqk', head_queries, head_keys, preferred_element_typ...  13.2 us
    all_to_all x1, waiting for transfers between devices, per_device(): lax.all_to_all(outgoing, ('view', 'seq'), split_axis=0, concat_axis=0, ti...  13.1 us
  transfers between devices with their start and end apart: 9, of which 3 were waited for; matrix products, arithmetic and copies ran while one was open for 26% of the time, Pallas kernels for 0%

commit v1 on v0

v1 whole, which is shorter than its diff:
```python
import functools
import math

import jax
import jax.numpy as jnp
from jax import lax
from jax.experimental import pallas as pl
from jax.experimental.pallas import tpu as pltpu
from jax.sharding import PartitionSpec as P

HEADS = 16
BLOCK = 128
GROUP = 128
NEGATIVE = -1e30
SHARPNESS_SCALE = 0.07
F32 = jnp.float32
BF16 = jnp.bfloat16


def remote(src, dst, send, recv, device):
    return pltpu.make_async_remote_copy(
        src_ref=src,
        dst_ref=dst,
        send_sem=send,
        recv_sem=recv,
        device_id=device,
        device_id_type=pl.DeviceIdType.MESH,
    )


def greet(devices):
    barrier = pltpu.get_barrier_semaphore()
    for device in devices:
        pl.semaphore_signal(
            barrier, inc=1, device_id=device, device_id_type=pl.DeviceIdType.MESH
        )
    pl.semaphore_wait(barrier, len(devices))


def attention_kernel(
    n_seq, head_dim, pattern, q_ref, k_ref, v_ref, mixed_ref,
    k_all, v_all, q_wide, best, total, accum,
    mate_send, mate_recv, row_send, row_recv, pass_send, pass_recv,
):
    points, width = q_ref.shape
    blocks = points // BLOCK
    groups = width // GROUP
    per_group = GROUP // head_dim
    rows = n_seq // 2
    me = lax.axis_index("seq")
    my_row, core = me // 2, me % 2
    mate = my_row * 2 + 1 - core
    mate_id = {"seq": mate}

    def row_peer(step):
        return lax.rem(my_row + step, rows) * 2 + core

    def row_source(step):
        return lax.rem(my_row + rows - step, rows)

    greet([mate_id] + [{"seq": row_peer(step)} for step in range(1, rows)])

    def key_row_copy(step, i):
        place = pl.ds(pl.multiple_of(i * BLOCK, BLOCK), BLOCK)
        return remote(
            k_ref.at[place], k_all.at[me, place],
            row_send.at[step - 1, 0, i], row_recv.at[step - 1, 0, i],
            {"seq": row_peer(step)},
        )

    def value_row_copy(step, i):
        return remote(
            v_all.at[me, i], v_all.at[me, i],
            row_send.at[step - 1, 1, i], row_recv.at[step - 1, 1, i],
            {"seq": row_peer(step)},
        )

    key_mate = remote(k_ref, k_all.at[me], mate_send.at[0], mate_recv.at[0], mate_id)
    value_mate = remote(
        v_all.at[me], v_all.at[me], mate_send.at[1], mate_recv.at[1], mate_id
    )

    key_row_copy(1, 0).start()
    for i in range(blocks):
        v_all[me, i] = v_ref[i * BLOCK : (i + 1) * BLOCK, :].T
        for step in range(1, rows):
            if step > 1 or i > 0:
                key_row_copy(step, i).start()
            value_row_copy(step, i).start()
    key_mate.start()
    value_mate.start()
    k_all[me] = k_ref[...]

    factor_in = head_dim ** (-0.5) * math.log2(math.e)
    q_wide[...] = jnp.zeros_like(q_wide)
    for b in range(blocks):
        turned = q_ref[b * BLOCK : (b + 1) * BLOCK, :].T.astype(F32) * factor_in
        high = turned.astype(BF16)
        low = (turned - high.astype(F32)).astype(BF16)
        for g in range(groups):
            for j in range(per_group):
                at = g * GROUP + j * head_dim
                cols = slice(j * BLOCK, (j + 1) * BLOCK)
                q_wide[b, g, j * head_dim : (j + 1) * head_dim, cols] = high[at : at + head_dim]
                q_wide[b, g, GROUP + j * head_dim : GROUP + (j + 1) * head_dim, cols] = low[
                    at : at + head_dim
                ]
    best[...] = jnp.full_like(best, NEGATIVE)
    total[...] = jnp.zeros_like(total)
    accum[...] = jnp.zeros_like(accum)

    def attend(source, i):
        place = pl.ds(pl.multiple_of(i * BLOCK, BLOCK), BLOCK)

        def one(b, carry):
            keep = pattern[b, source * blocks + i].astype(F32)
            bias = (keep - 1.0) * (-NEGATIVE)
            for g in range(groups):
                lanes = slice(g * GROUP, (g + 1) * GROUP)
                keys = k_all[source, place, lanes]
                scores = jnp.dot(
                    jnp.concatenate([keys, keys], axis=1), q_wide[b, g],
                    preferred_element_type=F32,
                )
                top = jnp.max(scores, axis=0, keepdims=True)
                old = best[b, g : g + 1]
                new = jnp.maximum(old, top + bias)
                weights = jnp.exp2(scores - jnp.maximum(old, top)).astype(BF16)
                fade = jnp.exp2(old - new)
                vals = v_all[source, i, lanes, :]
                vals = jnp.concatenate([vals, jnp.ones((16, BLOCK), BF16)], axis=0)
                vals = vals * keep.astype(BF16)
                out = jnp.dot(vals, weights, preferred_element_type=F32)
                best[b, g : g + 1] = new
                total[b, g : g + 1] = total[b, g : g + 1] * fade + out[GROUP : GROUP + 1]
                for j in range(per_group):
                    cols = slice(j * BLOCK, (j + 1) * BLOCK)
                    at = g * GROUP + j * head_dim
                    accum[b, at : at + head_dim] = (
                        accum[b, at : at + head_dim] * fade[:, cols]
                        + out[j * head_dim : (j + 1) * head_dim, cols]
                    )
            return carry

        lax.fori_loop(0, blocks, one, 0)

    lax.fori_loop(0, blocks, lambda i, c: (attend(me, i), c)[1], 0)
    remote(k_ref, k_all.at[mate], mate_send.at[0], mate_recv.at[0], mate_id).wait_recv()
    remote(
        v_all.at[mate], v_all.at[mate], mate_send.at[1], mate_recv.at[1], mate_id
    ).wait_recv()
    lax.fori_loop(0, blocks, lambda i, c: (attend(mate, i), c)[1], 0)

    for step in range(1, rows):
        origin = row_source(step) * 2
        near, far = origin + core, origin + 1 - core

        def arriving(i, carry, step=step, near=near, far=far):
            place = pl.ds(pl.multiple_of(i * BLOCK, BLOCK), BLOCK)
            remote(
                k_ref.at[place], k_all.at[near, place],
                row_send.at[step - 1, 0, i], row_recv.at[step - 1, 0, i], mate_id,
            ).wait_recv()
            remote(
                k_all.at[near, place], k_all.at[near, place],
                pass_send.at[step - 1, 0, i], pass_recv.at[step - 1, 0, i], mate_id,
            ).start()
            remote(
                v_all.at[near, i], v_all.at[near, i],
                row_send.at[step - 1, 1, i], row_recv.at[step - 1, 1, i], mate_id,
            ).wait_recv()
            remote(
                v_all.at[near, i], v_all.at[near, i],
                pass_send.at[step - 1, 1, i], pass_recv.at[step - 1, 1, i], mate_id,
            ).start()
            attend(near, i)
            remote(
                k_all.at[far, place], k_all.at[far, place],
                pass_send.at[step - 1, 0, i], pass_recv.at[step - 1, 0, i], mate_id,
            ).wait_recv()
            remote(
                v_all.at[far, i], v_all.at[far, i],
                pass_send.at[step - 1, 1, i], pass_recv.at[step - 1, 1, i], mate_id,
            ).wait_recv()
            attend(far, i)
            return carry

        lax.fori_loop(0, blocks, arriving, 0)

    for b in range(blocks):
        for g in range(groups):
            parts = []
            for j in range(per_group):
                at = g * GROUP + j * head_dim
                cols = slice(j * BLOCK, (j + 1) * BLOCK)
                parts.append(accum[b, at : at + head_dim] / total[b, g : g + 1, cols])
            mixed_ref[b * BLOCK : (b + 1) * BLOCK, g * GROUP : (g + 1) * GROUP] = (
                jnp.concatenate(parts, axis=0).T.astype(BF16)
            )

    key_mate.wait_send()
    value_mate.wait_send()
    for step in range(1, rows):
        near = row_source(step) * 2 + core
        for i in range(blocks):
            place = slice(i * BLOCK, (i + 1) * BLOCK)
            key_row_copy(step, i).wait_send()
            value_row_copy(step, i).wait_send()
            remote(
                k_all.at[near, place], k_all.at[near, place],
                pass_send.at[step - 1, 0, i], pass_recv.at[step - 1, 0, i], mate_id,
            ).wait_send()
            remote(
                v_all.at[near, i], v_all.at[near, i],
                pass_send.at[step - 1, 1, i], pass_recv.at[step - 1, 1, i], mate_id,
            ).wait_send()


def attention(pattern, queries, keys, values, n_seq):
    points, width = queries.shape
    head_dim = width // HEADS
    blocks = points // BLOCK
    groups = width // GROUP
    rows = n_seq // 2
    wide = GROUP // head_dim * BLOCK
    vmem = pl.BlockSpec(memory_space=pltpu.VMEM)
    hops = max(rows - 1, 1)
    return pl.pallas_call(
        functools.partial(attention_kernel, n_seq, head_dim),
        out_shape=jax.ShapeDtypeStruct((points, width), BF16),
        in_specs=[pl.BlockSpec(memory_space=pltpu.SMEM), vmem, vmem, vmem],
        out_specs=vmem,
        scratch_shapes=[
            pltpu.VMEM((n_seq, points, width), BF16),
            pltpu.VMEM((n_seq, blocks, width, BLOCK), BF16),
            pltpu.VMEM((blocks, groups, 2 * GROUP, wide), BF16),
            pltpu.VMEM((blocks, groups, wide), F32),
            pltpu.VMEM((blocks, groups, wide), F32),
            pltpu.VMEM((blocks, width, BLOCK), F32),
            pltpu.SemaphoreType.DMA((2,)),
            pltpu.SemaphoreType.DMA((2,)),
            pltpu.SemaphoreType.DMA((hops, 2, blocks)),
            pltpu.SemaphoreType.DMA((hops, 2, blocks)),
            pltpu.SemaphoreType.DMA((hops, 2, blocks)),
            pltpu.SemaphoreType.DMA((hops, 2, blocks)),
        ],
        compiler_params=pltpu.CompilerParams(
            collective_id=0, has_side_effects=True, vmem_limit_bytes=48 * 1024 * 1024
        ),
    )(pattern, queries, keys, values)


def contrast_kernel(
    n_seq, n_plane, n_event,
    mixed_ref, weight_ref, served_ref, rows_ref, slot_ref, live_ref,
    grad_ref, loss_ref,
    embed, outgoing, contenders, picks, logits, back_out, back_in,
    part_out, part_in, event_all, whole_all, plane_stat, event_stat,
    go_send, go_recv, back_send, back_recv, part_send, part_recv,
    event_send, event_recv, whole_send, whole_recv,
    pstat_send, pstat_recv, estat_send, estat_recv,
):
    points, width = mixed_ref.shape
    capacity = served_ref.shape[1]
    anchors_dev = rows_ref.shape[1]
    chunk = part_out.shape[1]
    me = lax.axis_index("view") * n_seq + lax.axis_index("seq")
    my_event = lax.axis_index("event")

    def plane_id(peer):
        return {"view": peer // n_seq, "seq": lax.rem(peer, n_seq)}

    def peer_at(step):
        return lax.rem(me + step, n_plane)

    def event_at(step):
        return lax.rem(my_event + step, n_event)

    greet(
        [plane_id(peer_at(step)) for step in range(1, n_plane)]
        + [{"event": event_at(step)} for step in range(1, n_event)]
    )
    others = [n_plane - step for step in range(1, n_plane)]

    def swap(src, dst, send, recv, peer, slot):
        return remote(src, dst.at[slot], send.at[peer], recv.at[slot], plane_id(peer))

    mixed = mixed_ref[...]
    embed[...] = jnp.dot(mixed, weight_ref[...], preferred_element_type=F32)
    rows = embed[...]
    inverse = lax.rsqrt(jnp.sum(rows * rows, axis=-1, keepdims=True) + 1e-06)
    unit = (rows * inverse).astype(BF16)

    point_index = lax.broadcasted_iota(jnp.int32, (points, capacity), 0)

    def pick_of(peer):
        return jnp.where(served_ref[pl.ds(peer, 1), :] == point_index, 1.0, 0.0)

    def gather(peer):
        pick = pick_of(peer).astype(BF16)
        picks[peer] = pick
        return jnp.dot(pick.T, unit, preferred_element_type=F32).astype(BF16)

    for step in others:
        peer = peer_at(step)
        outgoing[peer] = gather(peer)
        swap(outgoing.at[peer], contenders, go_send, go_recv, peer, me).start()
    contenders[me] = gather(me)

    anchor_pick = jnp.where(
        rows_ref[...] == lax.broadcasted_iota(jnp.int32, (points, anchors_dev), 0), 1.0, 0.0
    ).astype(BF16)
    anchors = jnp.dot(anchor_pick.T, unit, preferred_element_type=F32).astype(BF16)
    mixed_turned = mixed.T
    live = live_ref[...].astype(F32)
    slots = slot_ref[...]
    slot_index = lax.broadcasted_iota(jnp.int32, (capacity, anchors_dev), 0)

    def correct(peer):
        return jnp.where(slots - peer * capacity == slot_index, 1.0, 0.0)

    sums = jnp.zeros((1, anchors_dev), F32)
    goal = jnp.zeros((1, anchors_dev), F32)
    for step in [0] + [n_plane - s for s in others]:
        peer = peer_at(step)
        if step:
            swap(outgoing.at[peer], contenders, go_send, go_recv, peer, peer).wait_recv()
        scores = lax.dot_general(
            contenders[peer], anchors, (((1,), (1,)), ((), ())), preferred_element_type=F32
        ) / SHARPNESS_SCALE
        grown = jnp.exp(scores)
        logits[peer] = grown
        sums = sums + jnp.sum(grown, axis=0, keepdims=True)
        goal = goal + jnp.sum(scores * correct(peer), axis=0, keepdims=True)
    loss_part = jnp.sum(live * (jnp.log(sums) - goal), axis=1, keepdims=True)
    live_part = jnp.sum(live, axis=1, keepdims=True)
    row_index = lax.broadcasted_iota(jnp.int32, (8, 128), 0)
    plane_stat[me] = jnp.where(row_index == 0, loss_part, live_part)

    def grads_of(peer):
        return live * (logits[peer] / sums - correct(peer)) / SHARPNESS_SCALE

    def answer(peer):
        slopes = grads_of(peer).astype(BF16)
        return jnp.dot(slopes, anchors, preferred_element_type=F32).astype(BF16), slopes

    anchor_grads = jnp.zeros((anchors_dev, width), F32)
    for step in others:
        peer = peer_at(step)
        reply, slopes = answer(peer)
        back_out[peer] = reply
        swap(back_out.at[peer], back_in, back_send, back_recv, peer, me).start()
        swap(plane_stat.at[me], plane_stat, pstat_send, pstat_recv, peer, me).start()
        anchor_grads = anchor_grads + jnp.dot(
            slopes.T, contenders[peer], preferred_element_type=F32
        )
    reply, slopes = answer(me)
    back_in[me] = reply
    anchor_grads = anchor_grads + jnp.dot(slopes.T, contenders[me], preferred_element_type=F32)
    high = anchor_grads.astype(BF16)
    low = (anchor_grads - high.astype(F32)).astype(BF16)
    unit_grads = (
        jnp.dot(anchor_pick, high, preferred_element_type=F32)
        + jnp.dot(anchor_pick, low, preferred_element_type=F32)
        + jnp.dot(picks[me], back_in[me], preferred_element_type=F32)
    )
    for step in [n_plane - s for s in others]:
        peer = peer_at(step)
        swap(back_out.at[peer], back_in, back_send, back_recv, peer, peer).wait_recv()
        unit_grads = unit_grads + jnp.dot(
            picks[peer], back_in[peer], preferred_element_type=F32
        )
    rows = embed[...]
    inner = jnp.sum(rows * unit_grads, axis=-1, keepdims=True)
    embed_grads = (
        inverse * (unit_grads - rows * (inverse * inverse * inner))
    ).astype(BF16)
    part = jnp.dot(mixed_turned, embed_grads, preferred_element_type=F32).astype(BF16)
    for p in range(n_plane):
        part_out[p] = part[p * chunk : (p + 1) * chunk]

    for step in others:
        peer = peer_at(step)
        swap(part_out.at[peer], part_in, part_send, part_recv, peer, me).start()
    part_in[me] = part_out[me]
    for step in range(1, n_plane):
        peer = peer_at(step)
        swap(plane_stat.at[me], plane_stat, pstat_send, pstat_recv, peer, peer).wait_recv()
    stat = plane_stat[0]
    for p in range(1, n_plane):
        stat = stat + plane_stat[p]
    event_stat[my_event] = stat

    def event_swap(array, send, recv, step, slot):
        event = event_at(step)
        return remote(
            array.at[my_event], array.at[slot], send.at[event], recv.at[slot], {"event": event}
        )

    for step in range(1, n_event):
        event_swap(event_stat, estat_send, estat_recv, step, my_event).start()
    for step in range(1, n_plane):
        peer = peer_at(step)
        swap(part_out.at[peer], part_in, part_send, part_recv, peer, peer).wait_recv()
    reduced = part_in[0].astype(F32)
    for p in range(1, n_plane):
        reduced = reduced + part_in[p].astype(F32)
    event_all[my_event] = reduced.astype(BF16)
    for step in range(1, n_event):
        event_swap(event_all, event_send, event_recv, step, my_event).start()
    for step in range(1, n_event):
        event_swap(event_stat, estat_send, estat_recv, step, event_at(step)).wait_recv()
        event_swap(event_all, event_send, event_recv, step, event_at(step)).wait_recv()
    reduced = event_all[0].astype(F32)
    stat = event_stat[0]
    for e in range(1, n_event):
        reduced = reduced + event_all[e].astype(F32)
        stat = stat + event_stat[e]
    whole_all[me] = reduced.astype(BF16)
    for step in others:
        peer = peer_at(step)
        swap(whole_all.at[me], whole_all, whole_send, whole_recv, peer, me).start()
    loss_ref[0, 0] = jnp.max(stat[0:1] / stat[1:2])

    def unpack(p):
        grad_ref[pl.ds(pl.multiple_of(p * chunk, chunk), chunk), :] = whole_all[p].astype(F32)

    unpack(me)
    for step in [n_plane - s for s in others]:
        peer = peer_at(step)
        swap(whole_all.at[me], whole_all, whole_send, whole_recv, peer, peer).wait_recv()
        unpack(peer)

    for step in others:
        peer = peer_at(step)
        swap(outgoing.at[peer], contenders, go_send, go_recv, peer, me).wait_send()
        swap(back_out.at[peer], back_in, back_send, back_recv, peer, me).wait_send()
        swap(plane_stat.at[me], plane_stat, pstat_send, pstat_recv, peer, me).wait_send()
        swap(part_out.at[peer], part_in, part_send, part_recv, peer, me).wait_send()
        swap(whole_all.at[me], whole_all, whole_send, whole_recv, peer, me).wait_send()
    for step in range(1, n_event):
        event_swap(event_stat, estat_send, estat_recv, step, my_event).wait_send()
        event_swap(event_all, event_send, event_recv, step, my_event).wait_send()


def contrast(mixed, out_weight, served, rows, slots, live, n_seq, n_plane, n_event):
    points, width = mixed.shape
    senders, capacity = served.shape
    anchors_dev = rows.shape[1]
    chunk = width // n_plane
    vmem = pl.BlockSpec(memory_space=pltpu.VMEM)
    plane_sems = pltpu.SemaphoreType.DMA((n_plane,))
    event_sems = pltpu.SemaphoreType.DMA((n_event,))
    return pl.pallas_call(
        functools.partial(contrast_kernel, n_seq, n_plane, n_event),
        out_shape=(
            jax.ShapeDtypeStruct((width, width), F32),
            jax.ShapeDtypeStruct((1, 1), F32),
        ),
        in_specs=[vmem] * 6,
        out_specs=(vmem, pl.BlockSpec(memory_space=pltpu.SMEM)),
        scratch_shapes=[
            pltpu.VMEM((points, width), F32),
            pltpu.VMEM((senders, capacity, width), BF16),
            pltpu.VMEM((senders, capacity, width), BF16),
            pltpu.VMEM((senders, points, capacity), BF16),
            pltpu.VMEM((senders, capacity, anchors_dev), F32),
            pltpu.VMEM((senders, capacity, width), BF16),
            pltpu.VMEM((senders, capacity, width), BF16),
            pltpu.VMEM((n_plane, chunk, width), BF16),
            pltpu.VMEM((n_plane, chunk, width), BF16),
            pltpu.VMEM((n_event, chunk, width), BF16),
            pltpu.VMEM((n_plane, chunk, width), BF16),
            pltpu.VMEM((n_plane, 8, 128), F32),
            pltpu.VMEM((n_event, 8, 128), F32),
        ]
        + [plane_sems] * 6
        + [event_sems] * 2
        + [plane_sems] * 4
        + [event_sems] * 2,
        compiler_params=pltpu.CompilerParams(
            collective_id=1, has_side_effects=True, vmem_limit_bytes=48 * 1024 * 1024
        ),
    )(mixed, out_weight, served, rows, slots, live)


def per_device(
    query, key, value, pattern, out_weight, served, anchor_rows, positive_slot, anchor_live
):
    n_view, n_seq, n_event = (lax.axis_size(name) for name in ("view", "seq", "event"))
    mixed = attention(pattern[0, 0], query[0, 0], key[0, 0], value[0, 0], n_seq)
    grad, loss = contrast(
        mixed, out_weight, served[0, 0], anchor_rows[0], positive_slot[0], anchor_live[0],
        n_seq, n_view * n_seq, n_event,
    )
    return (mixed[None, None], grad, loss[0, 0])


def solution(mesh):
    placed = (
        P("event", "view", "seq", None),
        P("event", "view", "seq", None),
        P("event", "view", "seq", None),
        P("event", "view", "seq", None),
        P(),
        P("event", "view", "seq", None),
        P("event", "view", "seq"),
        P("event", "view", "seq"),
        P("event", "view", "seq"),
    )
    return jax.shard_map(
        per_device,
        mesh=mesh,
        in_specs=placed,
        out_specs=(P("event", "view", "seq", None), P(), P()),
        check_vma=False,
    )
```

time: 323 us -> 109 us (0.34)
  waiting for transfers between devices: 111 us -> 0 us
  Pallas kernels: 0 us -> 99.9 us
  matrix products: 59 us -> 0 us
  blocking collectives: 40.1 us -> 0 us
  local copies, waits for them, and re-layouts: 43.9 us -> 6.03 us
  other arithmetic: 37.4 us -> 0 us
  between operations: 16.9 us -> 2.46 us
  starting transfers between devices: 12.8 us -> 0 us
    pallas_call x0 -> x2, Pallas kernels: none -> 99.9 us  [the longest x1 51.5 us: contrast(): pl.pallas_call(functools.partial(contrast_kernel, n_seq, n_plane, n_event...]
    psum x1 -> x0, waiting for transfers between devices: 86.9 us -> none  [per_device(): lax.psum((loss_term, loss_part, live_part), ('view', 'seq', 'event'))]
    dot_general x42 -> x0, matrix products: 59 us -> none  [the longest x12 33.7 us: one_group(): jnp.einsum('hqk,khd->hqd', weights.astype(jnp.bfloat16), head_values, pre...]
    psum x1 -> x0, blocking collectives: 40.1 us -> none  [per_device(): lax.psum((loss_term, loss_part, live_part), ('view', 'seq', 'event'))]
    all_to_all x2 -> x0, waiting for transfers between devices: 23.7 us -> none  [the longest x1 13.1 us: per_device(): lax.all_to_all(outgoing, ('view', 'seq'), split_axis=0, concat_axis=0, ti...]
    dynamic_slice x48 -> x0, local copies, waits for them, and re-layouts: 19.4 us -> none  [attend(): lax.scan(one_group, state, (key_groups, value_groups, offsets))]
    reduce_sum x15 -> x0, other arithmetic: 16.5 us -> none  [the longest x12 15.1 us: one_group(): total = total * factor + jnp.sum(weights, axis=-1)]
    while x30 -> x0, local copies, waits for them, and re-layouts: 14.8 us -> none
  transfers between devices with their start and end apart: 9 -> 0, of which waited for: 3 -> 0; matrix products, arithmetic and copies ran while one was open for 26% -> 0% of each run, Pallas kernels for 0% -> 0%
where the time goes in v1:
time: 109 us; the launch traced here: 108 us
  Pallas kernels  99.9 us (92%)
  local copies, waits for them, and re-layouts  6.03 us (6%)
  between operations  2.46 us (2%)
    pallas_call x1, Pallas kernels, contrast(): pl.pallas_call(functools.partial(contrast_kernel, n_seq, n_plane, n_event...  51.5 us
    pallas_call x1, Pallas kernels, attention(): pl.pallas_call(functools.partial(attention_kernel, n_seq, head_dim), out_...  48.4 us
    unnamed x21, local copies, waits for them, and re-layouts  6.03 us

profile of v1, /device:TPU:0, one launch (start us, length us, event | category | flops | bytes accessed | tf_op | source)
XLA Modules:
  0.0 108.4 jit_solution(6973930927155909652)
XLA Ops:
  0.6 0.0 copy-start.8
  0.6 0.7 copy-done.8
  1.3 0.0 copy-start.1
  1.3 1.0 copy-done.1
  2.3 0.0 copy-start.2
  2.3 1.0 copy-done.2
  3.3 0.0 copy-start.3
  3.3 1.0 copy-done.3
  4.3 0.0 copy-start
  4.3 0.0 copy-start.4
  4.3 0.0 copy-start.6
  4.3 0.0 copy-start.7
  4.3 48.4 %shard_map.112.mixed_ref = bf16[384,512]{1,0:T(8,128)(2,1)S(1)} custom-call(s32[3,12]{1,0:T(4,128)S(1)} %bitcast.16, bf16[384,512]{1,0:T(8,128)(2,1)S(1)} %bitcast.13, bf16[384,512]{1,0:T(8,128)(2,1)S(1)} %bitcast.14, bf16[384,512]{1,0:T(8,128)(2,1)S(1)} %bitcast.15), custom_call_target="tpu_custom_call" | custom-call | tf_op jit(solution)/shard_map/pallas_call | solution.py:228
  52.7 0.0 copy-start.5
  52.7 0.0 copy-done
  52.7 0.0 copy-done.4
  52.7 0.0 copy-done.6
  52.7 0.0 copy-done.7
  52.7 0.6 copy-done.5
  53.4 51.5 %shard_map.113 = (f32[512,512]{1,0:T(8,128)S(1)}, f32[1,1]{1,0:T(1,128)}) custom-call(bf16[384,512]{1,0:T(8,128)(2,1)S(1)} %shard_map.112.mixed_ref, bf16[512,512]{1,0:T(8,128)(2,1)S(1)} %copy-done, s32[8,128]{1,0:T(8,128)S(1)} %bitcast.17, s32[1,256]{1,0:T(1,128)S(1)} %bitcast.18, s32[1,256]{1,0:T(1,128)S(1)} %bitcast.19, s32[1,256]{1,0:T(1,128)S(1)} %bitcast.20), custom_call_target="tpu_custom_call" | custom-call | tf_op jit(solution)/shard_map/pallas_call | solution.py:454
  104.9 0.7 copy.18
  105.7 1.0 copy.19
  (1 shorter events, 0.0 us)
Async XLA Ops:
  0.6 0.7 copy-start.8
  1.3 1.0 copy-start.1
  2.3 1.0 copy-start.2
  3.3 1.0 copy-start.3
  4.3 48.4 %copy-start = (bf16[512,512]{1,0:T(8,128)(2,1)S(1)}, bf16[512,512]{1,0:T(8,128)(2,1)}, u32[]{:S(2)}) copy-start(bf16[512,512]{1,0:T(8,128)(2,1)} %weight_ref.1) | copy-start | bytes 1572868
  4.3 48.4 %copy-start.4 = (s32[1,1,8,128]{3,2,1,0:T(8,128)S(1)}, s32[1,1,8,128]{3,2,1,0:T(8,128)}, u32[]{:S(2)}) copy-start(s32[1,1,8,128]{3,2,1,0:T(8,128)} %param.14) | copy-start | bytes 12292
  4.3 48.4 %copy-start.6 = (s32[1,1,256]{2,1,0:T(1,128)S(1)}, s32[1,1,256]{2,1,0:T(1,128)}, u32[]{:S(2)}) copy-start(s32[1,1,256]{2,1,0:T(1,128)} %param.16) | copy-start | bytes 3076
  4.3 48.4 %copy-start.7 = (s32[1,1,256]{2,1,0:T(1,128)S(1)}, s32[1,1,256]{2,1,0:T(1,128)}, u32[]{:S(2)}) copy-start(s32[1,1,256]{2,1,0:T(1,128)} %param.17) | copy-start | bytes 3076
  52.7 0.7 copy-start.5

commit v2 on v1

--- a/solution.py
+++ b/solution.py
@@ -109,47 +109,73 @@
     total[...] = jnp.zeros_like(total)
     accum[...] = jnp.zeros_like(accum)
 
-    def attend(source, i):
+    ones = jnp.ones((16, BLOCK), BF16)
+
+    def attend(first, second, i):
         place = pl.ds(pl.multiple_of(i * BLOCK, BLOCK), BLOCK)
-
-        def one(b, carry):
-            keep = pattern[b, source * blocks + i].astype(F32)
-            bias = (keep - 1.0) * (-NEGATIVE)
-            for g in range(groups):
-                lanes = slice(g * GROUP, (g + 1) * GROUP)
-                keys = k_all[source, place, lanes]
-                scores = jnp.dot(
-                    jnp.concatenate([keys, keys], axis=1), q_wide[b, g],
-                    preferred_element_type=F32,
+        sources = (first, second)
+        keeps = [
+            [pattern[b, source * blocks + i].astype(F32) for source in sources]
+            for b in range(blocks)
+        ]
+
+        def scores_of(b, g):
+            lanes = slice(g * GROUP, (g + 1) * GROUP)
+            keys = jnp.concatenate([k_all[source, place, lanes] for source in sources], axis=0)
+            return jnp.dot(
+                jnp.concatenate([keys, keys], axis=1), q_wide[b, g], preferred_element_type=F32
+            )
+
+        def finish(b, g, scores):
+            lanes = slice(g * GROUP, (g + 1) * GROUP)
+            halves = [scores[:BLOCK], scores[BLOCK:]]
+            tops = [jnp.max(half, axis=0, keepdims=True) for half in halves]
+            old = best[b, g : g + 1]
+            new = old
+            for top, keep in zip(tops, keeps[b]):
+                new = jnp.maximum(new, top + (keep - 1.0) * (-NEGATIVE))
+            weights = jnp.concatenate(
+                [
+                    jnp.exp2(half - jnp.maximum(new, top)).astype(BF16)
+                    for half, top in zip(halves, tops)
+                ],
+                axis=0,
+            )
+            fade = jnp.exp2(old - new)
+            best[b, g : g + 1] = new
+            vals = [
+                jnp.concatenate([v_all[source, i, lanes, :], ones], axis=0) * keep.astype(BF16)
+                for source, keep in zip(sources, keeps[b])
+            ]
+            vals = jnp.concatenate(vals, axis=1)
+            pair = 2 * head_dim
+            for n in range(per_group // 2):
+                cols = slice(2 * n * BLOCK, (2 * n + 2) * BLOCK)
+                rows_in = jnp.concatenate([vals[n * pair : (n + 1) * pair], vals[GROUP:]], axis=0)
+                out = jnp.dot(rows_in, weights[:, cols], preferred_element_type=F32)
+                total[b, g : g + 1, cols] = (
+                    total[b, g : g + 1, cols] * fade[:, cols] + out[pair : pair + 1]
                 )
-                top = jnp.max(scores, axis=0, keepdims=True)
-                old = best[b, g : g + 1]
-                new = jnp.maximum(old, top + bias)
-                weights = jnp.exp2(scores - jnp.maximum(old, top)).astype(BF16)
-                fade = jnp.exp2(old - new)
-                vals = v_all[source, i, lanes, :]
-                vals = jnp.concatenate([vals, jnp.ones((16, BLOCK), BF16)], axis=0)
-                vals = vals * keep.astype(BF16)
-                out = jnp.dot(vals, weights, preferred_element_type=F32)
-                best[b, g : g + 1] = new
-                total[b, g : g + 1] = total[b, g : g + 1] * fade + out[GROUP : GROUP + 1]
-                for j in range(per_group):
-                    cols = slice(j * BLOCK, (j + 1) * BLOCK)
-                    at = g * GROUP + j * head_dim
+                for j in range(2):
+                    at = g * GROUP + (2 * n + j) * head_dim
+                    side = slice(j * BLOCK, (j + 1) * BLOCK)
                     accum[b, at : at + head_dim] = (
-                        accum[b, at : at + head_dim] * fade[:, cols]
-                        + out[j * head_dim : (j + 1) * head_dim, cols]
+                        accum[b, at : at + head_dim] * fade[:, cols][:, side]
+                        + out[j * head_dim : (j + 1) * head_dim, side]
                     )
-            return carry
-
-        lax.fori_loop(0, blocks, one, 0)
-
-    lax.fori_loop(0, blocks, lambda i, c: (attend(me, i), c)[1], 0)
+
+        units = [(b, g) for b in range(blocks) for g in range(groups)]
+        ready = scores_of(*units[0])
+        for at, unit in enumerate(units):
+            later = scores_of(*units[at + 1]) if at + 1 < len(units) else None
+            finish(*unit, ready)
+            ready = later
+
     remote(k_ref, k_all.at[mate], mate_send.at[0], mate_recv.at[0], mate_id).wait_recv()
     remote(
         v_all.at[mate], v_all.at[mate], mate_send.at[1], mate_recv.at[1], mate_id
     ).wait_recv()
-    lax.fori_loop(0, blocks, lambda i, c: (attend(mate, i), c)[1], 0)
+    lax.fori_loop(0, blocks, lambda i, c: (attend(me, mate, i), c)[1], 0)
 
     for step in range(1, rows):
         origin = row_source(step) * 2
@@ -173,7 +199,6 @@
                 v_all.at[near, i], v_all.at[near, i],
                 pass_send.at[step - 1, 1, i], pass_recv.at[step - 1, 1, i], mate_id,
             ).start()
-            attend(near, i)
             remote(
                 k_all.at[far, place], k_all.at[far, place],
                 pass_send.at[step - 1, 0, i], pass_recv.at[step - 1, 0, i], mate_id,
@@ -182,7 +207,7 @@
                 v_all.at[far, i], v_all.at[far, i],
                 pass_send.at[step - 1, 1, i], pass_recv.at[step - 1, 1, i], mate_id,
             ).wait_recv()
-            attend(far, i)
+            attend(near, far, i)
             return carry
 
         lax.fori_loop(0, blocks, arriving, 0)
@@ -254,9 +279,9 @@
     n_seq, n_plane, n_event,
     mixed_ref, weight_ref, served_ref, rows_ref, slot_ref, live_ref,
     grad_ref, loss_ref,
-    embed, outgoing, contenders, picks, logits, back_out, back_in,
+    outgoing, contenders, direction, inverse, units, turned, logits, slopes, embed_grads,
     part_out, part_in, event_all, whole_all, plane_stat, event_stat,
-    go_send, go_recv, back_send, back_recv, part_send, part_recv,
+    go_send, go_recv, part_send, part_recv,
     event_send, event_recv, whole_send, whole_recv,
     pstat_send, pstat_recv, estat_send, estat_recv,
 ):
@@ -264,6 +289,7 @@
     capacity = served_ref.shape[1]
     anchors_dev = rows_ref.shape[1]
     chunk = part_out.shape[1]
+    cands = n_plane * capacity
     me = lax.axis_index("view") * n_seq + lax.axis_index("seq")
     my_event = lax.axis_index("event")
 
@@ -285,21 +311,11 @@
     def swap(src, dst, send, recv, peer, slot):
         return remote(src, dst.at[slot], send.at[peer], recv.at[slot], plane_id(peer))
 
-    mixed = mixed_ref[...]
-    embed[...] = jnp.dot(mixed, weight_ref[...], preferred_element_type=F32)
-    rows = embed[...]
-    inverse = lax.rsqrt(jnp.sum(rows * rows, axis=-1, keepdims=True) + 1e-06)
-    unit = (rows * inverse).astype(BF16)
-
     point_index = lax.broadcasted_iota(jnp.int32, (points, capacity), 0)
 
-    def pick_of(peer):
-        return jnp.where(served_ref[pl.ds(peer, 1), :] == point_index, 1.0, 0.0)
-
     def gather(peer):
-        pick = pick_of(peer).astype(BF16)
-        picks[peer] = pick
-        return jnp.dot(pick.T, unit, preferred_element_type=F32).astype(BF16)
+        pick = jnp.where(served_ref[pl.ds(peer, 1), :] == point_index, 1.0, 0.0).astype(BF16)
+        return jnp.dot(pick.T, mixed_ref[...], preferred_element_type=F32).astype(BF16)
 
     for step in others:
         peer = peer_at(step)
@@ -310,8 +326,20 @@
     anchor_pick = jnp.where(
         rows_ref[...] == lax.broadcasted_iota(jnp.int32, (points, anchors_dev), 0), 1.0, 0.0
     ).astype(BF16)
-    anchors = jnp.dot(anchor_pick.T, unit, preferred_element_type=F32).astype(BF16)
-    mixed_turned = mixed.T
+    anchor_mixed = jnp.dot(anchor_pick.T, mixed_ref[...], preferred_element_type=F32).astype(BF16)
+
+    def project(rows_mixed, at):
+        place = slice(at, at + rows_mixed.shape[0])
+        embed = jnp.dot(rows_mixed, weight_ref[...], preferred_element_type=F32)
+        scale = lax.rsqrt(jnp.sum(embed * embed, axis=-1, keepdims=True) + 1e-06)
+        embed = embed * scale
+        inverse[place] = scale
+        direction[place] = embed
+        units[place] = embed.astype(BF16)
+        turned[:, place] = rows_mixed.T
+
+    project(anchor_mixed, cands)
+    anchors = units[cands:]
     live = live_ref[...].astype(F32)
     slots = slot_ref[...]
     slot_index = lax.broadcasted_iota(jnp.int32, (capacity, anchors_dev), 0)
@@ -321,61 +349,47 @@
 
     sums = jnp.zeros((1, anchors_dev), F32)
     goal = jnp.zeros((1, anchors_dev), F32)
-    for step in [0] + [n_plane - s for s in others]:
+    arrivals = [0] + [n_plane - step for step in others]
+    for at, step in enumerate(arrivals):
         peer = peer_at(step)
         if step:
             swap(outgoing.at[peer], contenders, go_send, go_recv, peer, peer).wait_recv()
+        place = slice(at * capacity, (at + 1) * capacity)
+        project(contenders[peer], at * capacity)
         scores = lax.dot_general(
-            contenders[peer], anchors, (((1,), (1,)), ((), ())), preferred_element_type=F32
+            units[place], anchors, (((1,), (1,)), ((), ())), preferred_element_type=F32
         ) / SHARPNESS_SCALE
         grown = jnp.exp(scores)
-        logits[peer] = grown
+        logits[place] = grown
         sums = sums + jnp.sum(grown, axis=0, keepdims=True)
         goal = goal + jnp.sum(scores * correct(peer), axis=0, keepdims=True)
     loss_part = jnp.sum(live * (jnp.log(sums) - goal), axis=1, keepdims=True)
     live_part = jnp.sum(live, axis=1, keepdims=True)
     row_index = lax.broadcasted_iota(jnp.int32, (8, 128), 0)
     plane_stat[me] = jnp.where(row_index == 0, loss_part, live_part)
-
-    def grads_of(peer):
-        return live * (logits[peer] / sums - correct(peer)) / SHARPNESS_SCALE
-
-    def answer(peer):
-        slopes = grads_of(peer).astype(BF16)
-        return jnp.dot(slopes, anchors, preferred_element_type=F32).astype(BF16), slopes
-
-    anchor_grads = jnp.zeros((anchors_dev, width), F32)
     for step in others:
         peer = peer_at(step)
-        reply, slopes = answer(peer)
-        back_out[peer] = reply
-        swap(back_out.at[peer], back_in, back_send, back_recv, peer, me).start()
         swap(plane_stat.at[me], plane_stat, pstat_send, pstat_recv, peer, me).start()
-        anchor_grads = anchor_grads + jnp.dot(
-            slopes.T, contenders[peer], preferred_element_type=F32
-        )
-    reply, slopes = answer(me)
-    back_in[me] = reply
-    anchor_grads = anchor_grads + jnp.dot(slopes.T, contenders[me], preferred_element_type=F32)
-    high = anchor_grads.astype(BF16)
-    low = (anchor_grads - high.astype(F32)).astype(BF16)
-    unit_grads = (
-        jnp.dot(anchor_pick, high, preferred_element_type=F32)
-        + jnp.dot(anchor_pick, low, preferred_element_type=F32)
-        + jnp.dot(picks[me], back_in[me], preferred_element_type=F32)
-    )
-    for step in [n_plane - s for s in others]:
-        peer = peer_at(step)
-        swap(back_out.at[peer], back_in, back_send, back_recv, peer, peer).wait_recv()
-        unit_grads = unit_grads + jnp.dot(
-            picks[peer], back_in[peer], preferred_element_type=F32
-        )
-    rows = embed[...]
-    inner = jnp.sum(rows * unit_grads, axis=-1, keepdims=True)
-    embed_grads = (
-        inverse * (unit_grads - rows * (inverse * inverse * inner))
-    ).astype(BF16)
-    part = jnp.dot(mixed_turned, embed_grads, preferred_element_type=F32).astype(BF16)
+
+    for at, step in enumerate(arrivals):
+        place = slice(at * capacity, (at + 1) * capacity)
+        slopes[place] = (
+            live * (logits[place] / sums - correct(peer_at(step))) / SHARPNESS_SCALE
+        ).astype(BF16)
+
+    def pull_back(grads, place):
+        along = direction[place]
+        inner = jnp.sum(along * grads, axis=-1, keepdims=True)
+        embed_grads[place] = (inverse[place] * (grads - along * inner)).astype(BF16)
+
+    for at in range(0, cands, anchors_dev):
+        place = slice(at, at + anchors_dev)
+        pull_back(jnp.dot(slopes[place], anchors, preferred_element_type=F32), place)
+    pull_back(
+        jnp.dot(slopes[...].T, units[:cands], preferred_element_type=F32),
+        slice(cands, cands + anchors_dev),
+    )
+    part = jnp.dot(turned[...], embed_grads[...], preferred_element_type=F32).astype(BF16)
     for p in range(n_plane):
         part_out[p] = part[p * chunk : (p + 1) * chunk]
 
@@ -434,7 +448,6 @@
     for step in others:
         peer = peer_at(step)
         swap(outgoing.at[peer], contenders, go_send, go_recv, peer, me).wait_send()
-        swap(back_out.at[peer], back_in, back_send, back_recv, peer, me).wait_send()
         swap(plane_stat.at[me], plane_stat, pstat_send, pstat_recv, peer, me).wait_send()
         swap(part_out.at[peer], part_in, part_send, part_recv, peer, me).wait_send()
         swap(whole_all.at[me], whole_all, whole_send, whole_recv, peer, me).wait_send()
@@ -448,6 +461,8 @@
     senders, capacity = served.shape
     anchors_dev = rows.shape[1]
     chunk = width // n_plane
+    cands = senders * capacity
+    every = cands + anchors_dev
     vmem = pl.BlockSpec(memory_space=pltpu.VMEM)
     plane_sems = pltpu.SemaphoreType.DMA((n_plane,))
     event_sems = pltpu.SemaphoreType.DMA((n_event,))
@@ -460,13 +475,15 @@
         in_specs=[vmem] * 6,
         out_specs=(vmem, pl.BlockSpec(memory_space=pltpu.SMEM)),
         scratch_shapes=[
-            pltpu.VMEM((points, width), F32),
             pltpu.VMEM((senders, capacity, width), BF16),
             pltpu.VMEM((senders, capacity, width), BF16),
-            pltpu.VMEM((senders, points, capacity), BF16),
-            pltpu.VMEM((senders, capacity, anchors_dev), F32),
-            pltpu.VMEM((senders, capacity, width), BF16),
-            pltpu.VMEM((senders, capacity, width), BF16),
+            pltpu.VMEM((every, width), F32),
+            pltpu.VMEM((every, 1), F32),
+            pltpu.VMEM((every, width), BF16),
+            pltpu.VMEM((width, every), BF16),
+            pltpu.VMEM((cands, anchors_dev), F32),
+            pltpu.VMEM((cands, anchors_dev), BF16),
+            pltpu.VMEM((every, width), BF16),
             pltpu.VMEM((n_plane, chunk, width), BF16),
             pltpu.VMEM((n_plane, chunk, width), BF16),
             pltpu.VMEM((n_event, chunk, width), BF16),
@@ -474,7 +491,7 @@
             pltpu.VMEM((n_plane, 8, 128), F32),
             pltpu.VMEM((n_event, 8, 128), F32),
         ]
-        + [plane_sems] * 6
+        + [plane_sems] * 4
         + [event_sems] * 2
         + [plane_sems] * 4
         + [event_sems] * 2,

time: 109 us -> 73.9 us (0.68)
  Pallas kernels: 99.9 us -> 65.1 us
    pallas_call x1, Pallas kernels: 48.4 us -> 25.4 us  [attention(): pl.pallas_call(functools.partial(attention_kernel, n_seq, head_dim), out_...]
    pallas_call x1, Pallas kernels: 51.5 us -> 39.7 us  [contrast(): pl.pallas_call(functools.partial(contrast_kernel, n_seq, n_plane, n_event...]
where the time goes in v2:
time: 73.9 us; the launch traced here: 73.6 us
  Pallas kernels  65.1 us (88%)
  local copies, waits for them, and re-layouts  6.03 us (8%)
  between operations  2.46 us (3%)
    pallas_call x1, Pallas kernels, contrast(): pl.pallas_call(functools.partial(contrast_kernel, n_seq, n_plane, n_event...  39.7 us
    pallas_call x1, Pallas kernels, attention(): pl.pallas_call(functools.partial(attention_kernel, n_seq, head_dim), out_...  25.4 us
    unnamed x21, local copies, waits for them, and re-layouts  6.03 us

profile of v2, /device:TPU:0, one launch (start us, length us, event | category | flops | bytes accessed | tf_op | source)
XLA Modules:
  0.0 73.6 jit_solution(8515380812171320422)
XLA Ops:
  0.6 0.0 copy-start.8
  0.6 0.7 copy-done.8
  1.3 0.0 copy-start.1
  1.3 1.0 %copy-done.1 = bf16[1,1,384,512]{3,2,1,0:T(8,128)(2,1)S(1)} copy-done((bf16[1,1,384,512]{3,2,1,0:T(8,128)(2,1)S(1)}, bf16[1,1,384,512]{3,2,1,0:T(8,128)(2,1)}, u32[]{:S(2)}) %copy-start.1) | copy-done | bytes 393240
  2.3 0.0 copy-start.2
  2.3 1.0 %copy-done.2 = bf16[1,1,384,512]{3,2,1,0:T(8,128)(2,1)S(1)} copy-done((bf16[1,1,384,512]{3,2,1,0:T(8,128)(2,1)S(1)}, bf16[1,1,384,512]{3,2,1,0:T(8,128)(2,1)}, u32[]{:S(2)}) %copy-start.2) | copy-done | bytes 393240
  3.3 0.0 copy-start.3
  3.3 1.0 %copy-done.3 = bf16[1,1,384,512]{3,2,1,0:T(8,128)(2,1)S(1)} copy-done((bf16[1,1,384,512]{3,2,1,0:T(8,128)(2,1)S(1)}, bf16[1,1,384,512]{3,2,1,0:T(8,128)(2,1)}, u32[]{:S(2)}) %copy-start.3) | copy-done | bytes 393240
  4.3 0.0 copy-start
  4.3 0.0 copy-start.4
  4.3 0.0 copy-start.6
  4.3 0.0 copy-start.7
  4.3 25.4 %shard_map.112.mixed_ref = bf16[384,512]{1,0:T(8,128)(2,1)S(1)} custom-call(s32[3,12]{1,0:T(4,128)S(1)} %bitcast.16, bf16[384,512]{1,0:T(8,128)(2,1)S(1)} %bitcast.13, bf16[384,512]{1,0:T(8,128)(2,1)S(1)} %bitcast.14, bf16[384,512]{1,0:T(8,128)(2,1)S(1)} %bitcast.15), custom_call_target="tpu_custom_call" | custom-call | tf_op jit(solution)/shard_map/pallas_call | solution.py:253
  29.7 0.0 copy-start.5
  29.7 0.0 copy-done
  29.7 0.0 copy-done.4
  29.8 0.0 copy-done.6
  29.8 0.0 copy-done.7
  29.8 0.6 copy-done.5
  30.4 39.7 %shard_map.113 = (f32[512,512]{1,0:T(8,128)S(1)}, f32[1,1]{1,0:T(1,128)}) custom-call(bf16[384,512]{1,0:T(8,128)(2,1)S(1)} %shard_map.112.mixed_ref, bf16[512,512]{1,0:T(8,128)(2,1)S(1)} %copy-done, s32[8,128]{1,0:T(8,128)S(1)} %bitcast.17, s32[1,256]{1,0:T(1,128)S(1)} %bitcast.18, s32[1,256]{1,0:T(1,128)S(1)} %bitcast.19, s32[1,256]{1,0:T(1,128)S(1)} %bitcast.20), custom_call_target="tpu_custom_call" | custom-call | tf_op jit(solution)/shard_map/pallas_call | solution.py:469
  70.2 0.7 %copy.18 = bf16[1,1,384,512]{3,2,1,0:T(8,128)(2,1)} copy(bf16[1,1,384,512]{3,2,1,0:T(8,128)(2,1)S(1)} %bitcast.12) | data formatting | bytes 786432
  70.9 1.0 %copy.19 = f32[512,512]{1,0:T(8,128)} copy(f32[512,512]{1,0:T(8,128)S(1)} %get-tuple-element.11) | data formatting | bytes 2097152
  (1 shorter events, 0.0 us)
Async XLA Ops:
  0.6 0.7 copy-start.8
  1.3 1.0 %copy-start.1 = (bf16[1,1,384,512]{3,2,1,0:T(8,128)(2,1)S(1)}, bf16[1,1,384,512]{3,2,1,0:T(8,128)(2,1)}, u32[]{:S(2)}) copy-start(bf16[1,1,384,512]{3,2,1,0:T(8,128)(2,1)} %param.9) | copy-start | bytes 1179652
  2.3 1.0 %copy-start.2 = (bf16[1,1,384,512]{3,2,1,0:T(8,128)(2,1)S(1)}, bf16[1,1,384,512]{3,2,1,0:T(8,128)(2,1)}, u32[]{:S(2)}) copy-start(bf16[1,1,384,512]{3,2,1,0:T(8,128)(2,1)} %param.10) | copy-start | bytes 1179652
  3.3 1.0 %copy-start.3 = (bf16[1,1,384,512]{3,2,1,0:T(8,128)(2,1)S(1)}, bf16[1,1,384,512]{3,2,1,0:T(8,128)(2,1)}, u32[]{:S(2)}) copy-start(bf16[1,1,384,512]{3,2,1,0:T(8,128)(2,1)} %param.11) | copy-start | bytes 1179652
  4.3 25.4 %copy-start = (bf16[512,512]{1,0:T(8,128)(2,1)S(1)}, bf16[512,512]{1,0:T(8,128)(2,1)}, u32[]{:S(2)}) copy-start(bf16[512,512]{1,0:T(8,128)(2,1)} %weight_ref.1) | copy-start | bytes 1572868
  4.3 25.4 %copy-start.4 = (s32[1,1,8,128]{3,2,1,0:T(8,128)S(1)}, s32[1,1,8,128]{3,2,1,0:T(8,128)}, u32[]{:S(2)}) copy-start(s32[1,1,8,128]{3,2,1,0:T(8,128)} %param.14) | copy-start | bytes 12292
  4.3 25.4 %copy-start.6 = (s32[1,1,256]{2,1,0:T(1,128)S(1)}, s32[1,1,256]{2,1,0:T(1,128)}, u32[]{:S(2)}) copy-start(s32[1,1,256]{2,1,0:T(1,128)} %param.16) | copy-start | bytes 3076
  4.3 25.5 %copy-start.7 = (s32[1,1,256]{2,1,0:T(1,128)S(1)}, s32[1,1,256]{2,1,0:T(1,128)}, u32[]{:S(2)}) copy-start(s32[1,1,256]{2,1,0:T(1,128)} %param.17) | copy-start | bytes 3076
  29.7 0.7 copy-start.5

commit v3 on v2

--- a/solution.py
+++ b/solution.py
@@ -39,7 +39,7 @@
 
 def attention_kernel(
     n_seq, head_dim, pattern, q_ref, k_ref, v_ref, mixed_ref,
-    k_all, v_all, q_wide, best, total, accum,
+    q_in, v_in, k_all, v_all, q_wide, best, total, accum, load_sem,
     mate_send, mate_recv, row_send, row_recv, pass_send, pass_recv,
 ):
     points, width = q_ref.shape
@@ -58,6 +58,12 @@
     def row_source(step):
         return lax.rem(my_row + rows - step, rows)
 
+    loads = [
+        pltpu.make_async_copy(src, dst, load_sem.at[n])
+        for n, (src, dst) in enumerate(((v_ref, v_in), (q_ref, q_in), (k_ref, k_all.at[me])))
+    ]
+    for load in loads:
+        load.start()
     greet([mate_id] + [{"seq": row_peer(step)} for step in range(1, rows)])
 
     def key_row_copy(step, i):
@@ -81,20 +87,20 @@
     )
 
     key_row_copy(1, 0).start()
+    loads[0].wait()
     for i in range(blocks):
-        v_all[me, i] = v_ref[i * BLOCK : (i + 1) * BLOCK, :].T
+        v_all[me, i] = v_in[i * BLOCK : (i + 1) * BLOCK, :].T
         for step in range(1, rows):
             if step > 1 or i > 0:
                 key_row_copy(step, i).start()
             value_row_copy(step, i).start()
     key_mate.start()
     value_mate.start()
-    k_all[me] = k_ref[...]
-
+    loads[1].wait()
     factor_in = head_dim ** (-0.5) * math.log2(math.e)
     q_wide[...] = jnp.zeros_like(q_wide)
     for b in range(blocks):
-        turned = q_ref[b * BLOCK : (b + 1) * BLOCK, :].T.astype(F32) * factor_in
+        turned = q_in[b * BLOCK : (b + 1) * BLOCK, :].T.astype(F32) * factor_in
         high = turned.astype(BF16)
         low = (turned - high.astype(F32)).astype(BF16)
         for g in range(groups):
@@ -115,7 +121,7 @@
         place = pl.ds(pl.multiple_of(i * BLOCK, BLOCK), BLOCK)
         sources = (first, second)
         keeps = [
-            [pattern[b, source * blocks + i].astype(F32) for source in sources]
+            [pattern[b, 0, source * blocks + i].astype(F32) for source in sources]
             for b in range(blocks)
         ]
 
@@ -171,6 +177,7 @@
             finish(*unit, ready)
             ready = later
 
+    loads[2].wait()
     remote(k_ref, k_all.at[mate], mate_send.at[0], mate_recv.at[0], mate_id).wait_recv()
     remote(
         v_all.at[mate], v_all.at[mate], mate_send.at[1], mate_recv.at[1], mate_id
@@ -253,15 +260,18 @@
     return pl.pallas_call(
         functools.partial(attention_kernel, n_seq, head_dim),
         out_shape=jax.ShapeDtypeStruct((points, width), BF16),
-        in_specs=[pl.BlockSpec(memory_space=pltpu.SMEM), vmem, vmem, vmem],
+        in_specs=[pl.BlockSpec(memory_space=pltpu.SMEM)] + [pl.BlockSpec(memory_space=pltpu.HBM)] * 3,
         out_specs=vmem,
         scratch_shapes=[
+            pltpu.VMEM((points, width), BF16),
+            pltpu.VMEM((points, width), BF16),
             pltpu.VMEM((n_seq, points, width), BF16),
             pltpu.VMEM((n_seq, blocks, width, BLOCK), BF16),
             pltpu.VMEM((blocks, groups, 2 * GROUP, wide), BF16),
             pltpu.VMEM((blocks, groups, wide), F32),
             pltpu.VMEM((blocks, groups, wide), F32),
             pltpu.VMEM((blocks, width, BLOCK), F32),
+            pltpu.SemaphoreType.DMA((3,)),
             pltpu.SemaphoreType.DMA((2,)),
             pltpu.SemaphoreType.DMA((2,)),
             pltpu.SemaphoreType.DMA((hops, 2, blocks)),
@@ -270,7 +280,7 @@
             pltpu.SemaphoreType.DMA((hops, 2, blocks)),
         ],
         compiler_params=pltpu.CompilerParams(
-            collective_id=0, has_side_effects=True, vmem_limit_bytes=48 * 1024 * 1024
+            collective_id=0, has_side_effects=True, vmem_limit_bytes=63 * 1024 * 1024
         ),
     )(pattern, queries, keys, values)
 
@@ -280,7 +290,7 @@
     mixed_ref, weight_ref, served_ref, rows_ref, slot_ref, live_ref,
     grad_ref, loss_ref,
     outgoing, contenders, direction, inverse, units, turned, logits, slopes, embed_grads,
-    part_out, part_in, event_all, whole_all, plane_stat, event_stat,
+    part_out, part_in, event_all, plane_stat, event_stat,
     go_send, go_recv, part_send, part_recv,
     event_send, event_recv, whole_send, whole_recv,
     pstat_send, pstat_recv, estat_send, estat_recv,
@@ -288,28 +298,47 @@
     points, width = mixed_ref.shape
     capacity = served_ref.shape[1]
     anchors_dev = rows_ref.shape[1]
-    chunk = part_out.shape[1]
+    chunk = part_out.shape[2]
     cands = n_plane * capacity
-    me = lax.axis_index("view") * n_seq + lax.axis_index("seq")
+    n_view, n_row = n_plane // n_seq, n_seq // 2
+    my_view, my_seq = lax.axis_index("view"), lax.axis_index("seq")
+    my_row, my_core = my_seq // 2, my_seq % 2
+    me = my_view * n_seq + my_seq
     my_event = lax.axis_index("event")
 
-    def plane_id(peer):
-        return {"view": peer // n_seq, "seq": lax.rem(peer, n_seq)}
-
-    def peer_at(step):
-        return lax.rem(me + step, n_plane)
+    def seat(step, way):
+        view = lax.rem(my_view + n_view + way * step[0], n_view)
+        row = lax.rem(my_row + n_row + way * step[1], n_row)
+        core = lax.rem(my_core + 2 + way * step[2], 2)
+        return view, row * 2 + core
+
+    def target(step):
+        view, seq = seat(step, 1)
+        return view * n_seq + seq, {"view": view, "seq": seq}
+
+    def source(step):
+        view, seq = seat(step, -1)
+        return view * n_seq + seq
 
     def event_at(step):
         return lax.rem(my_event + step, n_event)
 
+    steps = [
+        (a, b, c) for a in range(n_view) for b in range(n_row) for c in range(2) if a or b or c
+    ]
+    steps.sort(key=lambda s: (-(s[0] > 0) - (s[1] > 0), s[2], s[0]))
     greet(
-        [plane_id(peer_at(step)) for step in range(1, n_plane)]
+        [target(step)[1] for step in steps]
         + [{"event": event_at(step)} for step in range(1, n_event)]
     )
-    others = [n_plane - step for step in range(1, n_plane)]
-
-    def swap(src, dst, send, recv, peer, slot):
-        return remote(src, dst.at[slot], send.at[peer], recv.at[slot], plane_id(peer))
+
+    def push(src, dst, send, recv, step):
+        peer, device = target(step)
+        return remote(src, dst.at[me], send.at[peer], recv.at[me], device)
+
+    def pull(dst, send, recv, step):
+        peer = source(step)
+        return remote(dst.at[peer], dst.at[peer], send.at[peer], recv.at[peer], target(step)[1])
 
     point_index = lax.broadcasted_iota(jnp.int32, (points, capacity), 0)
 
@@ -317,10 +346,10 @@
         pick = jnp.where(served_ref[pl.ds(peer, 1), :] == point_index, 1.0, 0.0).astype(BF16)
         return jnp.dot(pick.T, mixed_ref[...], preferred_element_type=F32).astype(BF16)
 
-    for step in others:
-        peer = peer_at(step)
+    for step in steps:
+        peer = target(step)[0]
         outgoing[peer] = gather(peer)
-        swap(outgoing.at[peer], contenders, go_send, go_recv, peer, me).start()
+        push(outgoing.at[peer], contenders, go_send, go_recv, step).start()
     contenders[me] = gather(me)
 
     anchor_pick = jnp.where(
@@ -349,11 +378,12 @@
 
     sums = jnp.zeros((1, anchors_dev), F32)
     goal = jnp.zeros((1, anchors_dev), F32)
-    arrivals = [0] + [n_plane - step for step in others]
+    arrivals = [None] + steps[-1:] + steps[:-1]
+    origins = [source(step) if step else me for step in arrivals]
     for at, step in enumerate(arrivals):
-        peer = peer_at(step)
+        peer = origins[at]
         if step:
-            swap(outgoing.at[peer], contenders, go_send, go_recv, peer, peer).wait_recv()
+            pull(contenders, go_send, go_recv, step).wait_recv()
         place = slice(at * capacity, (at + 1) * capacity)
         project(contenders[peer], at * capacity)
         scores = lax.dot_general(
@@ -367,14 +397,13 @@
     live_part = jnp.sum(live, axis=1, keepdims=True)
     row_index = lax.broadcasted_iota(jnp.int32, (8, 128), 0)
     plane_stat[me] = jnp.where(row_index == 0, loss_part, live_part)
-    for step in others:
-        peer = peer_at(step)
-        swap(plane_stat.at[me], plane_stat, pstat_send, pstat_recv, peer, me).start()
-
-    for at, step in enumerate(arrivals):
+    for step in steps:
+        push(plane_stat.at[me], plane_stat, pstat_send, pstat_recv, step).start()
+
+    for at, peer in enumerate(origins):
         place = slice(at * capacity, (at + 1) * capacity)
         slopes[place] = (
-            live * (logits[place] / sums - correct(peer_at(step))) / SHARPNESS_SCALE
+            live * (logits[place] / sums - correct(peer)) / SHARPNESS_SCALE
         ).astype(BF16)
 
     def pull_back(grads, place):
@@ -389,17 +418,19 @@
         jnp.dot(slopes[...].T, units[:cands], preferred_element_type=F32),
         slice(cands, cands + anchors_dev),
     )
-    part = jnp.dot(turned[...], embed_grads[...], preferred_element_type=F32).astype(BF16)
-    for p in range(n_plane):
-        part_out[p] = part[p * chunk : (p + 1) * chunk]
-
-    for step in others:
-        peer = peer_at(step)
-        swap(part_out.at[peer], part_in, part_send, part_recv, peer, me).start()
-    part_in[me] = part_out[me]
-    for step in range(1, n_plane):
-        peer = peer_at(step)
-        swap(plane_stat.at[me], plane_stat, pstat_send, pstat_recv, peer, peer).wait_recv()
+    parts = [slice(at, at + GROUP) for at in range(0, width, GROUP)]
+    for n, cols in enumerate(parts):
+        part = jnp.dot(turned[...], embed_grads[:, cols], preferred_element_type=F32)
+        part_out[n] = part.astype(BF16).reshape(n_plane, chunk, GROUP)
+        for step in steps:
+            peer = target(step)[0]
+            push(
+                part_out.at[n, peer], part_in.at[n], part_send.at[n], part_recv.at[n], step
+            ).start()
+        part_in[n, me] = part_out[n, me]
+
+    for step in steps:
+        pull(plane_stat, pstat_send, pstat_recv, step).wait_recv()
     stat = plane_stat[0]
     for p in range(1, n_plane):
         stat = stat + plane_stat[p]
@@ -413,47 +444,70 @@
 
     for step in range(1, n_event):
         event_swap(event_stat, estat_send, estat_recv, step, my_event).start()
-    for step in range(1, n_plane):
-        peer = peer_at(step)
-        swap(part_out.at[peer], part_in, part_send, part_recv, peer, peer).wait_recv()
-    reduced = part_in[0].astype(F32)
-    for p in range(1, n_plane):
-        reduced = reduced + part_in[p].astype(F32)
-    event_all[my_event] = reduced.astype(BF16)
-    for step in range(1, n_event):
-        event_swap(event_all, event_send, event_recv, step, my_event).start()
+
+    for n in range(len(parts)):
+        for step in steps:
+            pull(part_in.at[n], part_send.at[n], part_recv.at[n], step).wait_recv()
+        reduced = part_in[n, 0].astype(F32)
+        for p in range(1, n_plane):
+            reduced = reduced + part_in[n, p].astype(F32)
+        event_all[n, my_event] = reduced.astype(BF16)
+        for step in range(1, n_event):
+            event_swap(
+                event_all.at[n], event_send.at[n], event_recv.at[n], step, my_event
+            ).start()
+
+    def spread(n, cols, step):
+        peer, device = target(step)
+        mine = grad_ref.at[me, :, cols]
+        return remote(mine, mine, whole_send.at[n, peer], whole_recv.at[n, me], device)
+
+    def landed(n, cols, step):
+        peer = source(step)
+        theirs = grad_ref.at[peer, :, cols]
+        return remote(
+            theirs, theirs, whole_send.at[n, peer], whole_recv.at[n, peer], target(step)[1]
+        )
+
+    for n, cols in enumerate(parts):
+        for step in range(1, n_event):
+            event_swap(
+                event_all.at[n], event_send.at[n], event_recv.at[n], step, event_at(step)
+            ).wait_recv()
+        reduced = event_all[n, 0].astype(F32)
+        for e in range(1, n_event):
+            reduced = reduced + event_all[n, e].astype(F32)
+        grad_ref[me, :, cols] = reduced.astype(BF16)
+        for step in steps:
+            spread(n, cols, step).start()
+
     for step in range(1, n_event):
         event_swap(event_stat, estat_send, estat_recv, step, event_at(step)).wait_recv()
-        event_swap(event_all, event_send, event_recv, step, event_at(step)).wait_recv()
-    reduced = event_all[0].astype(F32)
     stat = event_stat[0]
     for e in range(1, n_event):
-        reduced = reduced + event_all[e].astype(F32)
         stat = stat + event_stat[e]
-    whole_all[me] = reduced.astype(BF16)
-    for step in others:
-        peer = peer_at(step)
-        swap(whole_all.at[me], whole_all, whole_send, whole_recv, peer, me).start()
     loss_ref[0, 0] = jnp.max(stat[0:1] / stat[1:2])
 
-    def unpack(p):
-        grad_ref[pl.ds(pl.multiple_of(p * chunk, chunk), chunk), :] = whole_all[p].astype(F32)
-
-    unpack(me)
-    for step in [n_plane - s for s in others]:
-        peer = peer_at(step)
-        swap(whole_all.at[me], whole_all, whole_send, whole_recv, peer, peer).wait_recv()
-        unpack(peer)
-
-    for step in others:
-        peer = peer_at(step)
-        swap(outgoing.at[peer], contenders, go_send, go_recv, peer, me).wait_send()
-        swap(plane_stat.at[me], plane_stat, pstat_send, pstat_recv, peer, me).wait_send()
-        swap(part_out.at[peer], part_in, part_send, part_recv, peer, me).wait_send()
-        swap(whole_all.at[me], whole_all, whole_send, whole_recv, peer, me).wait_send()
+    for step in steps:
+        peer = target(step)[0]
+        push(outgoing.at[peer], contenders, go_send, go_recv, step).wait_send()
+        push(plane_stat.at[me], plane_stat, pstat_send, pstat_recv, step).wait_send()
+        for n, cols in enumerate(parts):
+            push(
+                part_out.at[n, peer], part_in.at[n], part_send.at[n], part_recv.at[n], step
+            ).wait_send()
     for step in range(1, n_event):
         event_swap(event_stat, estat_send, estat_recv, step, my_event).wait_send()
-        event_swap(event_all, event_send, event_recv, step, my_event).wait_send()
+        for n in range(len(parts)):
+            event_swap(
+                event_all.at[n], event_send.at[n], event_recv.at[n], step, my_event
+            ).wait_send()
+    for n, cols in enumerate(parts):
+        for step in steps:
+            landed(n, cols, step).wait_recv()
+    for n, cols in enumerate(parts):
+        for step in steps:
+            spread(n, cols, step).wait_send()
 
 
 def contrast(mixed, out_weight, served, rows, slots, live, n_seq, n_plane, n_event):
@@ -464,12 +518,15 @@
     cands = senders * capacity
     every = cands + anchors_dev
     vmem = pl.BlockSpec(memory_space=pltpu.VMEM)
-    plane_sems = pltpu.SemaphoreType.DMA((n_plane,))
-    event_sems = pltpu.SemaphoreType.DMA((n_event,))
+    parts = width // GROUP
+
+    def sems(*dims):
+        return [pltpu.SemaphoreType.DMA(dims)] * 2
+
     return pl.pallas_call(
         functools.partial(contrast_kernel, n_seq, n_plane, n_event),
         out_shape=(
-            jax.ShapeDtypeStruct((width, width), F32),
+            jax.ShapeDtypeStruct((n_plane, chunk, width), BF16),
             jax.ShapeDtypeStruct((1, 1), F32),
         ),
         in_specs=[vmem] * 6,
@@ -484,19 +541,20 @@
             pltpu.VMEM((cands, anchors_dev), F32),
             pltpu.VMEM((cands, anchors_dev), BF16),
             pltpu.VMEM((every, width), BF16),
-            pltpu.VMEM((n_plane, chunk, width), BF16),
-            pltpu.VMEM((n_plane, chunk, width), BF16),
-            pltpu.VMEM((n_event, chunk, width), BF16),
-            pltpu.VMEM((n_plane, chunk, width), BF16),
+            pltpu.VMEM((parts, n_plane, chunk, GROUP), BF16),
+            pltpu.VMEM((parts, n_plane, chunk, GROUP), BF16),
+            pltpu.VMEM((parts, n_event, chunk, GROUP), BF16),
             pltpu.VMEM((n_plane, 8, 128), F32),
             pltpu.VMEM((n_event, 8, 128), F32),
         ]
-        + [plane_sems] * 4
-        + [event_sems] * 2
-        + [plane_sems] * 4
-        + [event_sems] * 2,
+        + sems(n_plane)
+        + sems(parts, n_plane)
+        + sems(parts, n_event)
+        + sems(parts, n_plane)
+        + sems(n_plane)
+        + sems(n_event),
         compiler_params=pltpu.CompilerParams(
-            collective_id=1, has_side_effects=True, vmem_limit_bytes=48 * 1024 * 1024
+            collective_id=1, has_side_effects=True, vmem_limit_bytes=40 * 1024 * 1024
         ),
     )(mixed, out_weight, served, rows, slots, live)
 
@@ -505,11 +563,12 @@
     query, key, value, pattern, out_weight, served, anchor_rows, positive_slot, anchor_live
 ):
     n_view, n_seq, n_event = (lax.axis_size(name) for name in ("view", "seq", "event"))
-    mixed = attention(pattern[0, 0], query[0, 0], key[0, 0], value[0, 0], n_seq)
+    mixed = attention(pattern[0].transpose(1, 0, 2), query[0, 0], key[0, 0], value[0, 0], n_seq)
     grad, loss = contrast(
         mixed, out_weight, served[0, 0], anchor_rows[0], positive_slot[0], anchor_live[0],
         n_seq, n_view * n_seq, n_event,
     )
+    grad = grad.reshape(out_weight.shape).astype(F32)
     return (mixed[None, None], grad, loss[0, 0])
 
 

time: 73.9 us -> 70.7 us (0.957)
  local copies, waits for them, and re-layouts: 6.03 us -> 2.39 us
  other arithmetic: 0 us -> 1.14 us
    unnamed x21 -> x13, local copies, waits for them, and re-layouts: 6.03 us -> 2.39 us
    pallas_call x1, Pallas kernels: 39.7 us -> 37.8 us  [contrast(): pl.pallas_call(functools.partial(contrast_kernel, n_seq, n_plane, n_event...]
    pallas_call x1, Pallas kernels: 25.4 us -> 26.6 us  [attention(): pl.pallas_call(functools.partial(attention_kernel, n_seq, head_dim), out_...]
    convert_element_type x0 -> x1, other arithmetic: none -> 1.14 us  [per_device(): grad = grad.reshape(out_weight.shape).astype(F32)]
where the time goes in v3:
time: 70.7 us; the launch traced here: 70.5 us
  Pallas kernels  64.4 us (91%)
  between operations  2.54 us (4%)
  local copies, waits for them, and re-layouts  2.39 us (3%)
  other arithmetic  1.14 us (2%)
    pallas_call x1, Pallas kernels, contrast(): pl.pallas_call(functools.partial(contrast_kernel, n_seq, n_plane, n_event...  37.8 us
    pallas_call x1, Pallas kernels, attention(): pl.pallas_call(functools.partial(attention_kernel, n_seq, head_dim), out_...  26.6 us
    unnamed x13, local copies, waits for them, and re-layouts  2.39 us

profile of v3, /device:TPU:0, one launch (start us, length us, event | category | flops | bytes accessed | tf_op | source)
XLA Modules:
  0.0 70.5 jit_solution(17774392977296004932)
XLA Ops:
  0.6 0.0 copy-start.1
  0.6 0.0 copy-start.2
  0.7 0.0 copy-start.4
  0.7 0.0 copy-start.5
  0.7 26.6 %shard_map.112.mixed_ref = bf16[384,512]{1,0:T(8,128)(2,1)} custom-call(s32[3,1,12]{2,1,0:T(1,128)} %bitcast.21, bf16[384,512]{1,0:T(8,128)(2,1)} %bitcast.18, bf16[384,512]{1,0:T(8,128)(2,1)} %bitcast.19, bf16[384,512]{1,0:T(8,128)(2,1)} %bitcast.20), custom_call_target="tpu_custom_call" | custom-call | tf_op jit(solution)/shard_map/pallas_call | solution.py:260
  27.3 0.0 copy-start.3
  27.3 0.0 copy-done.1
  27.3 0.0 copy-done.2
  27.3 0.0 copy-done.4
  27.4 0.0 copy-done.5
  27.4 0.6 copy-done.3
  28.0 0.0 copy-start
  28.0 1.0 %copy-done = bf16[384,512]{1,0:T(8,128)(2,1)S(1)} copy-done((bf16[384,512]{1,0:T(8,128)(2,1)S(1)}, bf16[384,512]{1,0:T(8,128)(2,1)}, u32[]{:S(2)}) %copy-start) | copy-done | bytes 393240
  29.0 37.8 %shard_map.113 = (bf16[8,64,512]{2,1,0:T(8,128)(2,1)S(1)}, f32[1,1]{1,0:T(1,128)}) custom-call(bf16[384,512]{1,0:T(8,128)(2,1)S(1)} %copy-done, bf16[512,512]{1,0:T(8,128)(2,1)S(1)} %copy-done.1, s32[8,128]{1,0:T(8,128)S(1)} %bitcast.14, s32[1,256]{1,0:T(1,128)S(1)} %bitcast.15, s32[1,256]{1,0:T(1,128)S(1)} %bitcast.16, s32[1,256]{1,0:T(1,128)S(1)} %bitcast.17), custom_call_target="tpu_custom_call" | custom-call | tf_op jit(solution)/shard_map/pallas_call | solution.py:526
  66.8 1.1 %bitcast_convert_fusion = f32[512,512]{1,0:T(8,128)} fusion(bf16[8,64,512]{2,1,0:T(8,128)(2,1)S(1)} %get-tuple-element.5), kind=kLoop, calls=%fused_computation | loop fusion | flops 262144 | bytes 1572864 | tf_op jit(solution)/shard_map/convert_element_type | solution.py:571
  67.9 0.7 %copy.14 = bf16[1,1,384,512]{3,2,1,0:T(8,128)(2,1)} copy(bf16[1,1,384,512]{3,2,1,0:T(8,128)(2,1)S(1)} %bitcast.13) | data formatting | bytes 786432
Async XLA Ops:
  0.6 26.7 %copy-start.1 = (bf16[512,512]{1,0:T(8,128)(2,1)S(1)}, bf16[512,512]{1,0:T(8,128)(2,1)}, u32[]{:S(2)}) copy-start(bf16[512,512]{1,0:T(8,128)(2,1)} %weight_ref.1) | copy-start | bytes 1572868
  0.6 26.7 %copy-start.2 = (s32[1,1,8,128]{3,2,1,0:T(8,128)S(1)}, s32[1,1,8,128]{3,2,1,0:T(8,128)}, u32[]{:S(2)}) copy-start(s32[1,1,8,128]{3,2,1,0:T(8,128)} %param.14) | copy-start | bytes 12292
  0.7 26.7 %copy-start.4 = (s32[1,1,256]{2,1,0:T(1,128)S(1)}, s32[1,1,256]{2,1,0:T(1,128)}, u32[]{:S(2)}) copy-start(s32[1,1,256]{2,1,0:T(1,128)} %param.16) | copy-start | bytes 3076
  0.7 26.7 %copy-start.5 = (s32[1,1,256]{2,1,0:T(1,128)S(1)}, s32[1,1,256]{2,1,0:T(1,128)}, u32[]{:S(2)}) copy-start(s32[1,1,256]{2,1,0:T(1,128)} %param.17) | copy-start | bytes 3076
  27.3 0.7 copy-start.3
  28.0 1.0 %copy-start = (bf16[384,512]{1,0:T(8,128)(2,1)S(1)}, bf16[384,512]{1,0:T(8,128)(2,1)}, u32[]{:S(2)}) copy-start(bf16[384,512]{1,0:T(8,128)(2,1)} %shard_map.112.mixed_ref) | copy-start | bytes 1179652

commit v4 on v3

--- a/solution.py
+++ b/solution.py
@@ -37,8 +37,39 @@
     pl.semaphore_wait(barrier, len(devices))
 
 
-def attention_kernel(
-    n_seq, head_dim, pattern, q_ref, k_ref, v_ref, mixed_ref,
+def seats(n_seq, n_plane, n_event):
+    n_view, n_row = n_plane // n_seq, n_seq // 2
+    my_view, my_seq = lax.axis_index("view"), lax.axis_index("seq")
+    my_row, my_core = my_seq // 2, my_seq % 2
+    me = my_view * n_seq + my_seq
+    my_event = lax.axis_index("event")
+
+    def seat(step, way):
+        view = lax.rem(my_view + n_view + way * step[0], n_view)
+        row = lax.rem(my_row + n_row + way * step[1], n_row)
+        core = lax.rem(my_core + 2 + way * step[2], 2)
+        return view, row * 2 + core
+
+    def target(step):
+        view, seq = seat(step, 1)
+        return view * n_seq + seq, {"view": view, "seq": seq}
+
+    def source(step):
+        view, seq = seat(step, -1)
+        return view * n_seq + seq
+
+    def event_at(step):
+        return lax.rem(my_event + step, n_event)
+
+    steps = [
+        (a, b, c) for a in range(n_view) for b in range(n_row) for c in range(2) if a or b or c
+    ]
+    steps.sort(key=lambda s: (-(s[0] > 0) - (s[1] > 0), s[2], s[0]))
+    return my_event, me, target, source, event_at, steps
+
+
+def attend_part(
+    n_seq, head_dim, arrive, pattern, q_ref, k_ref, v_ref, mixed_ref,
     q_in, v_in, k_all, v_all, q_wide, best, total, accum, load_sem,
     mate_send, mate_recv, row_send, row_recv, pass_send, pass_recv,
 ):
@@ -64,7 +95,7 @@
     ]
     for load in loads:
         load.start()
-    greet([mate_id] + [{"seq": row_peer(step)} for step in range(1, rows)])
+    arrive()
 
     def key_row_copy(step, i):
         place = pl.ds(pl.multiple_of(i * BLOCK, BLOCK), BLOCK)
@@ -222,10 +253,11 @@
     for b in range(blocks):
         for g in range(groups):
             parts = []
+            share = 1.0 / total[b, g : g + 1]
             for j in range(per_group):
                 at = g * GROUP + j * head_dim
                 cols = slice(j * BLOCK, (j + 1) * BLOCK)
-                parts.append(accum[b, at : at + head_dim] / total[b, g : g + 1, cols])
+                parts.append(accum[b, at : at + head_dim] * share[:, cols])
             mixed_ref[b * BLOCK : (b + 1) * BLOCK, g * GROUP : (g + 1) * GROUP] = (
                 jnp.concatenate(parts, axis=0).T.astype(BF16)
             )
@@ -248,46 +280,8 @@
             ).wait_send()
 
 
-def attention(pattern, queries, keys, values, n_seq):
-    points, width = queries.shape
-    head_dim = width // HEADS
-    blocks = points // BLOCK
-    groups = width // GROUP
-    rows = n_seq // 2
-    wide = GROUP // head_dim * BLOCK
-    vmem = pl.BlockSpec(memory_space=pltpu.VMEM)
-    hops = max(rows - 1, 1)
-    return pl.pallas_call(
-        functools.partial(attention_kernel, n_seq, head_dim),
-        out_shape=jax.ShapeDtypeStruct((points, width), BF16),
-        in_specs=[pl.BlockSpec(memory_space=pltpu.SMEM)] + [pl.BlockSpec(memory_space=pltpu.HBM)] * 3,
-        out_specs=vmem,
-        scratch_shapes=[
-            pltpu.VMEM((points, width), BF16),
-            pltpu.VMEM((points, width), BF16),
-            pltpu.VMEM((n_seq, points, width), BF16),
-            pltpu.VMEM((n_seq, blocks, width, BLOCK), BF16),
-            pltpu.VMEM((blocks, groups, 2 * GROUP, wide), BF16),
-            pltpu.VMEM((blocks, groups, wide), F32),
-            pltpu.VMEM((blocks, groups, wide), F32),
-            pltpu.VMEM((blocks, width, BLOCK), F32),
-            pltpu.SemaphoreType.DMA((3,)),
-            pltpu.SemaphoreType.DMA((2,)),
-            pltpu.SemaphoreType.DMA((2,)),
-            pltpu.SemaphoreType.DMA((hops, 2, blocks)),
-            pltpu.SemaphoreType.DMA((hops, 2, blocks)),
-            pltpu.SemaphoreType.DMA((hops, 2, blocks)),
-            pltpu.SemaphoreType.DMA((hops, 2, blocks)),
-        ],
-        compiler_params=pltpu.CompilerParams(
-            collective_id=0, has_side_effects=True, vmem_limit_bytes=63 * 1024 * 1024
-        ),
-    )(pattern, queries, keys, values)
-
-
-def contrast_kernel(
-    n_seq, n_plane, n_event,
-    mixed_ref, weight_ref, served_ref, rows_ref, slot_ref, live_ref,
+def contrast_part(
+    n_seq, n_plane, n_event, early, mixed_ref, weight_ref, served_ref, rows_ref, slot_ref, live_ref,
     grad_ref, loss_ref,
     outgoing, contenders, direction, inverse, units, turned, logits, slopes, embed_grads,
     part_out, part_in, event_all, plane_stat, event_stat,
@@ -300,37 +294,7 @@
     anchors_dev = rows_ref.shape[1]
     chunk = part_out.shape[2]
     cands = n_plane * capacity
-    n_view, n_row = n_plane // n_seq, n_seq // 2
-    my_view, my_seq = lax.axis_index("view"), lax.axis_index("seq")
-    my_row, my_core = my_seq // 2, my_seq % 2
-    me = my_view * n_seq + my_seq
-    my_event = lax.axis_index("event")
-
-    def seat(step, way):
-        view = lax.rem(my_view + n_view + way * step[0], n_view)
-        row = lax.rem(my_row + n_row + way * step[1], n_row)
-        core = lax.rem(my_core + 2 + way * step[2], 2)
-        return view, row * 2 + core
-
-    def target(step):
-        view, seq = seat(step, 1)
-        return view * n_seq + seq, {"view": view, "seq": seq}
-
-    def source(step):
-        view, seq = seat(step, -1)
-        return view * n_seq + seq
-
-    def event_at(step):
-        return lax.rem(my_event + step, n_event)
-
-    steps = [
-        (a, b, c) for a in range(n_view) for b in range(n_row) for c in range(2) if a or b or c
-    ]
-    steps.sort(key=lambda s: (-(s[0] > 0) - (s[1] > 0), s[2], s[0]))
-    greet(
-        [target(step)[1] for step in steps]
-        + [{"event": event_at(step)} for step in range(1, n_event)]
-    )
+    my_event, me, target, source, event_at, steps = early
 
     def push(src, dst, send, recv, step):
         peer, device = target(step)
@@ -369,6 +333,7 @@
 
     project(anchor_mixed, cands)
     anchors = units[cands:]
+    anchors_turned = anchors.T
     live = live_ref[...].astype(F32)
     slots = slot_ref[...]
     slot_index = lax.broadcasted_iota(jnp.int32, (capacity, anchors_dev), 0)
@@ -386,9 +351,8 @@
             pull(contenders, go_send, go_recv, step).wait_recv()
         place = slice(at * capacity, (at + 1) * capacity)
         project(contenders[peer], at * capacity)
-        scores = lax.dot_general(
-            units[place], anchors, (((1,), (1,)), ((), ())), preferred_element_type=F32
-        ) / SHARPNESS_SCALE
+        scores = jnp.dot(units[place], anchors_turned, preferred_element_type=F32)
+        scores = scores * (1.0 / SHARPNESS_SCALE)
         grown = jnp.exp(scores)
         logits[place] = grown
         sums = sums + jnp.sum(grown, axis=0, keepdims=True)
@@ -400,11 +364,11 @@
     for step in steps:
         push(plane_stat.at[me], plane_stat, pstat_send, pstat_recv, step).start()
 
+    pull_up = live * (1.0 / SHARPNESS_SCALE)
+    share = pull_up / sums
     for at, peer in enumerate(origins):
         place = slice(at * capacity, (at + 1) * capacity)
-        slopes[place] = (
-            live * (logits[place] / sums - correct(peer)) / SHARPNESS_SCALE
-        ).astype(BF16)
+        slopes[place] = (logits[place] * share - correct(peer) * pull_up).astype(BF16)
 
     def pull_back(grads, place):
         along = direction[place]
@@ -510,63 +474,125 @@
             spread(n, cols, step).wait_send()
 
 
-def contrast(mixed, out_weight, served, rows, slots, live, n_seq, n_plane, n_event):
-    points, width = mixed.shape
-    senders, capacity = served.shape
-    anchors_dev = rows.shape[1]
-    chunk = width // n_plane
-    cands = senders * capacity
-    every = cands + anchors_dev
-    vmem = pl.BlockSpec(memory_space=pltpu.VMEM)
-    parts = width // GROUP
-
-    def sems(*dims):
-        return [pltpu.SemaphoreType.DMA(dims)] * 2
-
-    return pl.pallas_call(
-        functools.partial(contrast_kernel, n_seq, n_plane, n_event),
-        out_shape=(
-            jax.ShapeDtypeStruct((n_plane, chunk, width), BF16),
-            jax.ShapeDtypeStruct((1, 1), F32),
-        ),
-        in_specs=[vmem] * 6,
-        out_specs=(vmem, pl.BlockSpec(memory_space=pltpu.SMEM)),
-        scratch_shapes=[
-            pltpu.VMEM((senders, capacity, width), BF16),
-            pltpu.VMEM((senders, capacity, width), BF16),
-            pltpu.VMEM((every, width), F32),
-            pltpu.VMEM((every, 1), F32),
-            pltpu.VMEM((every, width), BF16),
-            pltpu.VMEM((width, every), BF16),
-            pltpu.VMEM((cands, anchors_dev), F32),
-            pltpu.VMEM((cands, anchors_dev), BF16),
-            pltpu.VMEM((every, width), BF16),
-            pltpu.VMEM((parts, n_plane, chunk, GROUP), BF16),
-            pltpu.VMEM((parts, n_plane, chunk, GROUP), BF16),
-            pltpu.VMEM((parts, n_event, chunk, GROUP), BF16),
-            pltpu.VMEM((n_plane, 8, 128), F32),
-            pltpu.VMEM((n_event, 8, 128), F32),
-        ]
-        + sems(n_plane)
-        + sems(parts, n_plane)
-        + sems(parts, n_event)
-        + sems(parts, n_plane)
-        + sems(n_plane)
-        + sems(n_event),
-        compiler_params=pltpu.CompilerParams(
-            collective_id=1, has_side_effects=True, vmem_limit_bytes=40 * 1024 * 1024
-        ),
-    )(mixed, out_weight, served, rows, slots, live)
+def whole_kernel(
+    n_seq, n_plane, n_event, head_dim, n_attend,
+    pattern, q_ref, k_ref, v_ref, weight_hbm, served_hbm, rows_hbm, slot_hbm, live_hbm,
+    mixed_ref, grad_ref, loss_ref,
+    weight_ref, served_ref, rows_ref, slot_ref, live_ref, input_sem, *scratch,
+):
+    early = seats(n_seq, n_plane, n_event)
+    my_event, me, target, source, event_at, steps = early
+    pairs = (
+        (weight_hbm, weight_ref), (served_hbm, served_ref), (rows_hbm, rows_ref),
+        (slot_hbm, slot_ref), (live_hbm, live_ref),
+    )
+    inputs = [
+        pltpu.make_async_copy(src, dst, input_sem.at[n]) for n, (src, dst) in enumerate(pairs)
+    ]
+
+    def arrive():
+        for load in inputs:
+            load.start()
+        greet(
+            [target(step)[1] for step in steps]
+            + [{"event": event_at(step)} for step in range(1, n_event)]
+        )
+
+    attend_part(
+        n_seq, head_dim, arrive, pattern, q_ref, k_ref, v_ref, mixed_ref, *scratch[:n_attend]
+    )
+    for load in inputs:
+        load.wait()
+    contrast_part(
+        n_seq, n_plane, n_event, early, mixed_ref, weight_ref, served_ref, rows_ref, slot_ref,
+        live_ref, grad_ref, loss_ref, *scratch[n_attend:],
+    )
 
 
 def per_device(
     query, key, value, pattern, out_weight, served, anchor_rows, positive_slot, anchor_live
 ):
     n_view, n_seq, n_event = (lax.axis_size(name) for name in ("view", "seq", "event"))
-    mixed = attention(pattern[0].transpose(1, 0, 2), query[0, 0], key[0, 0], value[0, 0], n_seq)
-    grad, loss = contrast(
-        mixed, out_weight, served[0, 0], anchor_rows[0], positive_slot[0], anchor_live[0],
-        n_seq, n_view * n_seq, n_event,
+    n_plane = n_view * n_seq
+    points, width = query.shape[2:]
+    senders, capacity = served.shape[2:]
+    anchors_dev = anchor_rows.shape[2]
+    head_dim = width // HEADS
+    blocks = points // BLOCK
+    groups = width // GROUP
+    wide = GROUP // head_dim * BLOCK
+    hops = max(n_seq // 2 - 1, 1)
+    chunk = width // n_plane
+    cands = senders * capacity
+    every = cands + anchors_dev
+    parts = width // GROUP
+    dma = pltpu.SemaphoreType.DMA
+
+    def sems(*dims):
+        return [dma(dims)] * 2
+
+    inputs = [
+        pltpu.VMEM((width, width), BF16),
+        pltpu.VMEM((senders, capacity), jnp.int32),
+        pltpu.VMEM((1, anchors_dev), jnp.int32),
+        pltpu.VMEM((1, anchors_dev), jnp.int32),
+        pltpu.VMEM((1, anchors_dev), jnp.int32),
+        dma((5,)),
+    ]
+    attend = [
+        pltpu.VMEM((points, width), BF16),
+        pltpu.VMEM((points, width), BF16),
+        pltpu.VMEM((n_seq, points, width), BF16),
+        pltpu.VMEM((n_seq, blocks, width, BLOCK), BF16),
+        pltpu.VMEM((blocks, groups, 2 * GROUP, wide), BF16),
+        pltpu.VMEM((blocks, groups, wide), F32),
+        pltpu.VMEM((blocks, groups, wide), F32),
+        pltpu.VMEM((blocks, width, BLOCK), F32),
+        dma((3,)),
+        *sems(2),
+        *sems(hops, 2, blocks),
+        *sems(hops, 2, blocks),
+    ]
+    contrast = [
+        pltpu.VMEM((senders, capacity, width), BF16),
+        pltpu.VMEM((senders, capacity, width), BF16),
+        pltpu.VMEM((every, width), F32),
+        pltpu.VMEM((every, 1), F32),
+        pltpu.VMEM((every, width), BF16),
+        pltpu.VMEM((width, every), BF16),
+        pltpu.VMEM((cands, anchors_dev), F32),
+        pltpu.VMEM((cands, anchors_dev), BF16),
+        pltpu.VMEM((every, width), BF16),
+        pltpu.VMEM((parts, n_plane, chunk, GROUP), BF16),
+        pltpu.VMEM((parts, n_plane, chunk, GROUP), BF16),
+        pltpu.VMEM((parts, n_event, chunk, GROUP), BF16),
+        pltpu.VMEM((n_plane, 8, 128), F32),
+        pltpu.VMEM((n_event, 8, 128), F32),
+        *sems(n_plane),
+        *sems(parts, n_plane),
+        *sems(parts, n_event),
+        *sems(parts, n_plane),
+        *sems(n_plane),
+        *sems(n_event),
+    ]
+    smem = pl.BlockSpec(memory_space=pltpu.SMEM)
+    vmem = pl.BlockSpec(memory_space=pltpu.VMEM)
+    mixed, grad, loss = pl.pallas_call(
+        functools.partial(whole_kernel, n_seq, n_plane, n_event, head_dim, len(attend)),
+        out_shape=(
+            jax.ShapeDtypeStruct((points, width), BF16),
+            jax.ShapeDtypeStruct((n_plane, chunk, width), BF16),
+            jax.ShapeDtypeStruct((1, 1), F32),
+        ),
+        in_specs=[smem] + [pl.BlockSpec(memory_space=pltpu.HBM)] * 8,
+        out_specs=(vmem, vmem, smem),
+        scratch_shapes=inputs + attend + contrast,
+        compiler_params=pltpu.CompilerParams(
+            collective_id=0, has_side_effects=True, vmem_limit_bytes=63 * 1024 * 1024
+        ),
+    )(
+        pattern[0].transpose(1, 0, 2), query[0, 0], key[0, 0], value[0, 0], out_weight,
+        served[0, 0], anchor_rows[0], positive_slot[0], anchor_live[0],
     )
     grad = grad.reshape(out_weight.shape).astype(F32)
     return (mixed[None, None], grad, loss[0, 0])

time: 70.7 us -> 68.6 us (0.970)
  local copies, waits for them, and re-layouts: 2.39 us -> 0.75 us
  Pallas kernels: 64.4 us -> 63.1 us
  other arithmetic: 1.14 us -> 2.2 us
    unnamed x13 -> x3, local copies, waits for them, and re-layouts: 2.39 us -> 0.75 us
    pallas_call x2 -> x1, Pallas kernels: 64.4 us -> 63.1 us  [per_device(): pl.pallas_call(functools.partial(whole_kernel, n_seq, n_plane, n_event, h...]
    convert_element_type x1, other arithmetic: 1.14 us -> 2.2 us  [per_device(): grad = grad.reshape(out_weight.shape).astype(F32)]
where the time goes in v4:
time: 68.6 us; the launch traced here: 68.4 us
  Pallas kernels  63.1 us (92%)
  between operations  2.4 us (3%)
  other arithmetic  2.2 us (3%)
  local copies, waits for them, and re-layouts  0.75 us (1%)
    pallas_call x1, Pallas kernels, per_device(): pl.pallas_call(functools.partial(whole_kernel, n_seq, n_plane, n_event, h...  63.1 us
    convert_element_type x1, other arithmetic, per_device(): grad = grad.reshape(out_weight.shape).astype(F32)  2.2 us

profile of v4, /device:TPU:0, one launch (start us, length us, event | category | flops | bytes accessed | tf_op | source)
XLA Modules:
  0.0 68.4 jit_solution(2369313370878699187)
XLA Ops:
  0.6 63.1 %shard_map.112 = (bf16[384,512]{1,0:T(8,128)(2,1)}, bf16[8,64,512]{2,1,0:T(8,128)(2,1)}, f32[1,1]{1,0:T(1,128)}) custom-call(s32[3,1,12]{2,1,0:T(1,128)} %bitcast.18, bf16[384,512]{1,0:T(8,128)(2,1)} %bitcast.14, bf16[384,512]{1,0:T(8,128)(2,1)} %bitcast.15, bf16[384,512]{1,0:T(8,128)(2,1)} %bitcast.16, bf16[512,512]{1,0:T(8,128)(2,1)} %weight_hbm.1, ...), custom_call_target="tpu_custom_call" | custom-call | tf_op jit(solution)/shard_map/pallas_call | solution.py:580
  63.7 0.0 copy-start
  63.7 2.2 %bitcast_convert_fusion = f32[512,512]{1,0:T(8,128)} fusion(bf16[8,64,512]{2,1,0:T(8,128)(2,1)} %get-tuple-element.7), kind=kLoop, calls=%fused_computation | loop fusion | flops 262144 | bytes 1572864 | tf_op jit(solution)/shard_map/convert_element_type | solution.py:597
  65.9 0.0 copy-done
  65.9 0.7 %copy.14 = bf16[1,1,384,512]{3,2,1,0:T(8,128)(2,1)} copy(bf16[1,1,384,512]{3,2,1,0:T(8,128)(2,1)S(1)} %bitcast.13) | data formatting | bytes 786432
Async XLA Ops:
  63.7 2.2 %copy-start = (bf16[384,512]{1,0:T(8,128)(2,1)S(1)}, bf16[384,512]{1,0:T(8,128)(2,1)}, u32[]{:S(2)}) copy-start(bf16[384,512]{1,0:T(8,128)(2,1)} %get-tuple-element.6) | copy-start | bytes 1179652

commit v5 on v4

--- a/solution.py
+++ b/solution.py
@@ -421,6 +421,17 @@
                 event_all.at[n], event_send.at[n], event_recv.at[n], step, my_event
             ).start()
 
+    mate_step = (0, 0, 1)
+    same_core = [step for step in steps if step[2] == 0]
+
+    def hand_over(n, cols, step):
+        block = source(step)
+        ref = grad_ref.at[block, :, cols]
+        slot = target((step[0], step[1], 1))[0]
+        return remote(
+            ref, ref, whole_send.at[n, slot], whole_recv.at[n, block], target(mate_step)[1]
+        )
+
     def spread(n, cols, step):
         peer, device = target(step)
         mine = grad_ref.at[me, :, cols]
@@ -442,8 +453,13 @@
         for e in range(1, n_event):
             reduced = reduced + event_all[n, e].astype(F32)
         grad_ref[me, :, cols] = reduced.astype(BF16)
-        for step in steps:
+        for step in same_core + [mate_step]:
             spread(n, cols, step).start()
+
+    for n, cols in enumerate(parts):
+        for step in same_core:
+            landed(n, cols, step).wait_recv()
+            hand_over(n, cols, step).start()
 
     for step in range(1, n_event):
         event_swap(event_stat, estat_send, estat_recv, step, event_at(step)).wait_recv()
@@ -468,10 +484,13 @@
             ).wait_send()
     for n, cols in enumerate(parts):
         for step in steps:
-            landed(n, cols, step).wait_recv()
+            if step[2]:
+                landed(n, cols, step).wait_recv()
     for n, cols in enumerate(parts):
-        for step in steps:
+        for step in same_core + [mate_step]:
             spread(n, cols, step).wait_send()
+        for step in same_core:
+            hand_over(n, cols, step).wait_send()
 
 
 def whole_kernel(

time: 68.6 us -> 69.2 us (level)
  no operation moved by 1% of the time
where the time goes in v5:
time: 69.2 us; the launch traced here: 69 us
  Pallas kernels  63.7 us (92%)
  between operations  2.4 us (3%)
  other arithmetic  2.2 us (3%)
  local copies, waits for them, and re-layouts  0.75 us (1%)
    pallas_call x1, Pallas kernels, per_device(): pl.pallas_call(functools.partial(whole_kernel, n_seq, n_plane, n_event, h...  63.7 us
    convert_element_type x1, other arithmetic, per_device(): grad = grad.reshape(out_weight.shape).astype(F32)  2.2 us

profile of v5, /device:TPU:0, one launch (start us, length us, event | category | flops | bytes accessed | tf_op | source)
XLA Modules:
  0.0 69.0 jit_solution(7095512674954445154)
XLA Ops:
  0.6 63.7 %shard_map.112 = (bf16[384,512]{1,0:T(8,128)(2,1)}, bf16[8,64,512]{2,1,0:T(8,128)(2,1)}, f32[1,1]{1,0:T(1,128)}) custom-call(s32[3,1,12]{2,1,0:T(1,128)} %bitcast.18, bf16[384,512]{1,0:T(8,128)(2,1)} %bitcast.14, bf16[384,512]{1,0:T(8,128)(2,1)} %bitcast.15, bf16[384,512]{1,0:T(8,128)(2,1)} %bitcast.16, bf16[512,512]{1,0:T(8,128)(2,1)} %weight_hbm.1, ...), custom_call_target="tpu_custom_call" | custom-call | tf_op jit(solution)/shard_map/pallas_call | solution.py:599
  64.3 0.0 copy-start
  64.3 2.2 %bitcast_convert_fusion = f32[512,512]{1,0:T(8,128)} fusion(bf16[8,64,512]{2,1,0:T(8,128)(2,1)} %get-tuple-element.7), kind=kLoop, calls=%fused_computation | loop fusion | flops 262144 | bytes 1572864 | tf_op jit(solution)/shard_map/convert_element_type | solution.py:616
  66.5 0.0 copy-done
  66.5 0.7 %copy.14 = bf16[1,1,384,512]{3,2,1,0:T(8,128)(2,1)} copy(bf16[1,1,384,512]{3,2,1,0:T(8,128)(2,1)S(1)} %bitcast.13) | data formatting | bytes 786432
Async XLA Ops:
  64.3 2.2 %copy-start = (bf16[384,512]{1,0:T(8,128)(2,1)S(1)}, bf16[384,512]{1,0:T(8,128)(2,1)}, u32[]{:S(2)}) copy-start(bf16[384,512]{1,0:T(8,128)(2,1)} %get-tuple-element.6) | copy-start | bytes 1179652
